TPU v7x, 256 devices: a whole 4x4x8 slice. The times are simulated.
256 devices in a mesh: grp: 8 (over z), leaf: 32 (over y, x, core).
Axes of the slice: x: 4, y: 4, z: 8, core: 2. Of those that a mesh axis runs over, the one named last changes fastest.
Arguments:
- configs: bfloat16 [524288, 64], P(('grp', 'leaf')), may hold values from -6 to 6, as said below
- order: int32 [256, 2048], P(('grp', 'leaf')), may hold values from 0 to 2047, each once within a row
- w_in: bfloat16 [64, 128], replicated, may hold values from -0.75 to 0.75
- bias_in: float32 [128], replicated, may hold values from -3 to 3
- w_out: bfloat16 [128, 128], replicated, may hold values from -0.5 to 0.5
- noise: float32 [524288], P(('grp', 'leaf')), may hold values from 0.2 to 2
- right_side: float32 [524288], P(('grp', 'leaf')), may hold values from -12 to 12, as said below
- near_blocks: int32 [2048, 6], P(('grp', 'leaf')), may hold values from 0 to 255
- near_live: int32 [2048, 6], P(('grp', 'leaf')), may hold values 0 or 1
- skeleton: int32 [8, 256], P('grp'), may hold values from 0 to 65535
Outputs:
- solution: float32 [524288], P(('grp', 'leaf'))
- residual: float32 [524288], P(('grp', 'leaf'))
Inputs may be any that keep to these rules, and one draw needn't show every extreme that they name: `configs`: configurations of order one. `right_side`: targets of order one.
All inputs are finite; a program needn't handle non-finite values. No bound on the sum of `near_live` on one device may be relied on, other than what follows from the above.
Results may differ from a plain program's by a relative error of at most 0.039.
Values may be sent and summed in bfloat16 or wider, within the bound.
A program may use at most 128 MiB of HBM per device.

v0:
```python
import jax
import jax.numpy as jnp
from jax import lax
from jax.sharding import PartitionSpec as P

BLK = 256
NEAR = 6
ITERS = 4


sharpness = 10.0
highest = lax.Precision.HIGHEST


def kernel_rows(left, right):
    inner = lax.dot_general(
        left, right, (((1,), (1,)), ((), ())), preferred_element_type=jnp.float32
    )
    return jnp.exp(sharpness * (inner - 1.0))


def features_of(inputs, w_in, bias_in, w_out):
    hidden = jnp.tanh(jnp.dot(inputs, w_in, preferred_element_type=jnp.float32) + bias_in).astype(
        jnp.bfloat16
    )
    raw = jnp.dot(hidden, w_out, preferred_element_type=jnp.float32)
    return (raw * lax.rsqrt(jnp.sum(raw * raw, -1, keepdims=True) + 1e-06)).astype(jnp.bfloat16)


def near_tiles(inputs):
    own_feat, part_feat, own_vec, part_vec, weights, out_weight = inputs
    self_tile = kernel_rows(own_feat, own_feat)
    cross = jnp.exp(
        sharpness
        * (jnp.einsum("if,kjf->kij", own_feat, part_feat, preferred_element_type=jnp.float32) - 1.0)
    )
    partner_tile = jnp.exp(
        sharpness
        * (
            jnp.einsum("kif,kjf->kij", part_feat, part_feat, preferred_element_type=jnp.float32)
            - 1.0
        )
    )
    own_out = out_weight * jnp.dot(self_tile, own_vec, precision=highest)
    own_out = own_out + jnp.sum(
        weights[:, None] * jnp.einsum("kij,kj->ki", cross, part_vec, precision=highest), 0
    )
    back = jnp.einsum("kij,i->kj", cross, own_vec, precision=highest) + jnp.einsum(
        "kij,kj->ki", partner_tile, part_vec, precision=highest
    )
    return (own_out, weights[:, None] * back)


def on_device(
    configs, order, w_in, bias_in, w_out, noise, right_side, near_blocks, near_live, skeleton
):
    row_count = configs.shape[0]
    blocks_dev = row_count // BLK
    tree_rows = jnp.take(configs, order[0], axis=0)
    own_features = features_of(tree_rows, w_in, bias_in, w_out)
    group_feat = lax.all_gather(own_features, "leaf", axis=0, tiled=True)
    group_blocks = group_feat.shape[0] // BLK
    skel_feat = jnp.take(group_feat, skeleton[0], axis=0)
    all_skel = lax.all_gather(skel_feat, "grp", axis=0, tiled=True)
    basis = kernel_rows(own_features, skel_feat)
    coupling = kernel_rows(skel_feat, all_skel)
    live_mask = near_live.astype(jnp.float32)
    out_weights = jnp.sum(live_mask, 1)
    flat_partners = near_blocks.reshape(-1)
    part_feat = jnp.take(group_feat.reshape(group_blocks, BLK, -1), flat_partners, axis=0).reshape(
        blocks_dev, NEAR, BLK, -1
    )
    own_blocks = own_features.reshape(blocks_dev, BLK, -1)
    picker = (jnp.arange(group_blocks, dtype=jnp.int32)[:, None] == flat_partners[None, :]).astype(
        jnp.float32
    )
    precond = 1.0 / (1.0 + noise)
    solution = jnp.zeros_like(right_side)
    residual = right_side

    def inner_total(left, right):
        return lax.psum(jnp.sum(left * right), ("grp", "leaf"))

    scaled = residual * precond
    direction = scaled
    product_now = inner_total(residual, scaled)
    for step in range(ITERS):
        whole = lax.all_gather(direction, "leaf", axis=0, tiled=True)
        part_vec = jnp.take(whole.reshape(group_blocks, BLK), near_blocks, axis=0)
        own_out, back = lax.map(
            near_tiles,
            (
                own_blocks,
                part_feat,
                direction.reshape(blocks_dev, BLK),
                part_vec,
                live_mask,
                out_weights,
            ),
        )
        back_flat = back.reshape(-1, BLK)
        returned = lax.psum_scatter(
            jnp.dot(picker, back_flat, precision=highest).astype(jnp.bfloat16),
            "leaf",
            scatter_dimension=0,
            tiled=True,
        ).astype(jnp.float32)
        apply_local_charge = jnp.dot(direction, basis, precision=highest)
        group_total = lax.psum(apply_local_charge, "leaf")
        charges = lax.all_gather(group_total[None, :], "grp", axis=0, tiled=True)
        field = jnp.dot(coupling, charges.reshape(-1), precision=highest)
        far_part = jnp.dot(basis, field, precision=highest)
        image = (own_out + returned).reshape(-1) + far_part + noise * direction
        step_size = product_now / inner_total(direction, image)
        solution = solution + step_size * direction
        residual = residual - step_size * image
        if step + 1 < ITERS:
            scaled = residual * precond
            product_next = inner_total(residual, scaled)
            direction = scaled + product_next / product_now * direction
            product_now = product_next
    return (solution, residual)


def solution(mesh):
    in_specs = (
        P(("grp", "leaf"), None),
        P(("grp", "leaf"), None),
        P(),
        P(),
        P(),
        P(("grp", "leaf")),
        P(("grp", "leaf")),
        P(("grp", "leaf"), None),
        P(("grp", "leaf"), None),
        P("grp", None),
    )
    out_specs = (P(("grp", "leaf")), P(("grp", "leaf")))
    return jax.shard_map(
        on_device, mesh=mesh, in_specs=in_specs, out_specs=out_specs, check_vma=False
    )
```

profile of v0, /device:TPU:1, one launch (start us, length us, event | category | flops | bytes accessed | tf_op | source)
XLA Modules:
  0.0 1393.7 jit_solution(11065837192118993395)
XLA Ops:
  18.3 26.4 %all_gather.31 = f32[65536]{0:T(1024)S(1)} all-gather(f32[2048]{0:T(1024)S(1)} %fusion.156), channel_id=1, replica_groups=mesh['grp'=8,'leaf'=32] {'leaf'}, dimensions={0}, use_global_device_ids=true | all-gather | bytes 270336 | tf_op jit(solution)/shard_map/all_gather | solution.py:88
  45.9 54.2 %all-gather.6.cloned.1.call-done = bf16[65536,128]{1,0:T(8,128)(2,1)} async-done(((bf16[2048,128]{1,0:T(8,128)(2,1)}), bf16[65536,128]{1,0:T(8,128)(2,1)}) %all-gather.6.cloned.1.call-update) | async-done | bytes 16777232 | tf_op jit(solution)/shard_map/all_gather | solution.py:61
  110.7 20.9 %all_gather.32 = bf16[2048,128]{1,0:T(8,128)(2,1)S(1)} all-gather(bf16[256,128]{1,0:T(8,128)(2,1)S(1)} %broadcast_select_fusion.1), channel_id=1, replica_groups=mesh['grp'=8,'leaf'=32] {'grp'}, dimensions={0}, use_global_device_ids=true | all-gather | bytes 589824 | tf_op jit(solution)/shard_map/all_gather | solution.py:64
  144.0 71.0 %while.60 = (s32[]{:T(128)}, f32[8,256]{1,0:T(8,128)S(1)}, f32[8,6,256]{2,1,0:T(8,128)S(1)}, f32[8]{0:T(128)S(1)}, bf16[8,256,128]{2,1,0:T(8,128)(2,1)S(1)}, /*i...) while((s32[]{:T(128)}, f32[8,256]{1,0:T(8,128)S(1)}, ...), condition=%wide.region_6.8_spmd, body=%wide.region_4.7_spmd.sunk | while | flops 234756352 | bytes 9386733 | solution.py:90
  218.7 68.4 %psum.85 = f32[1,256]{1,0:T(1,128)S(1)} all-reduce(f32[1,256]{1,0:T(1,128)S(1)} %fusion.159), channel_id=1, replica_groups=mesh['grp'=8,'leaf'=32] {'leaf'}, use_global_device_ids=true, to_apply=%region_8.10 | all-reduce | flops 256 | bytes 2048 | tf_op jit(solution)/shard_map/psum | solution.py:109
  287.1 11.3 all-gather
  304.9 74.9 %all-reduce = (f32[]{:T(128)}, f32[]{:T(128)}) all-reduce(f32[]{:T(128)} %get-tuple-element.568, f32[]{:T(128)} %get-tuple-element.567), channel_id=1, replica_groups=mesh['grp'=8,'leaf'=32] {'grp','leaf'}, use_global_device_ids=true, to_apply=%region_1.2 | all-reduce | flops 2 | bytes 16 | tf_op jit(solution)/shard_map/psum | solution.py:82
  381.7 74.4 %psum.87 = f32[]{:T(128)} all-reduce(f32[]{:T(128)} %get-tuple-element.647), channel_id=1, replica_groups=mesh['grp'=8,'leaf'=32] {'grp','leaf'}, use_global_device_ids=true, to_apply=%region_12.14 | all-reduce | flops 1 | bytes 8 | tf_op jit(solution)/shard_map/psum | solution.py:82
  457.5 25.0 %all_gather.34 = f32[65536]{0:T(1024)S(1)} all-gather(f32[2048]{0:T(1024)S(1)} %multiply_add_fusion.10), channel_id=1, replica_groups=mesh['grp'=8,'leaf'=32] {'leaf'}, dimensions={0}, use_global_device_ids=true | all-gather | bytes 270336 | tf_op jit(solution)/shard_map/all_gather | solution.py:88
  483.3 70.9 %while.61 = (s32[]{:T(128)}, f32[8,256]{1,0:T(8,128)S(1)}, f32[8,6,256]{2,1,0:T(8,128)S(1)}, f32[8]{0:T(128)S(1)}, bf16[8,256,128]{2,1,0:T(8,128)(2,1)S(1)}, /*i...) while((s32[]{:T(128)}, f32[8,256]{1,0:T(8,128)S(1)}, ...), condition=%wide.region_15.17_spmd, body=%wide.region_13.16_spmd.sunk | while | flops 234756352 | bytes 9386733 | solution.py:90
  557.8 62.3 %psum.88 = f32[1,256]{1,0:T(1,128)S(1)} all-reduce(f32[1,256]{1,0:T(1,128)S(1)} %fusion.161), channel_id=1, replica_groups=mesh['grp'=8,'leaf'=32] {'leaf'}, use_global_device_ids=true, to_apply=%region_17.19 | all-reduce | flops 256 | bytes 2048 | tf_op jit(solution)/shard_map/psum | solution.py:109
  620.1 10.8 all-gather.1
  637.5 77.4 %psum.89 = f32[]{:T(128)} all-reduce(f32[]{:T(128)} %multiply_reduce_fusion.5), channel_id=1, replica_groups=mesh['grp'=8,'leaf'=32] {'grp','leaf'}, use_global_device_ids=true, to_apply=%region_19.21 | all-reduce | flops 1 | bytes 8 | tf_op jit(solution)/shard_map/psum | solution.py:82
  716.8 74.3 %psum.90 = f32[]{:T(128)} all-reduce(f32[]{:T(128)} %get-tuple-element.645), channel_id=1, replica_groups=mesh['grp'=8,'leaf'=32] {'grp','leaf'}, use_global_device_ids=true, to_apply=%region_21.23 | all-reduce | flops 1 | bytes 8 | tf_op jit(solution)/shard_map/psum | solution.py:82
  792.5 25.3 %all_gather.36 = f32[65536]{0:T(1024)S(1)} all-gather(f32[2048]{0:T(1024)S(1)} %multiply_add_fusion.8), channel_id=1, replica_groups=mesh['grp'=8,'leaf'=32] {'leaf'}, dimensions={0}, use_global_device_ids=true | all-gather | bytes 270336 | tf_op jit(solution)/shard_map/all_gather | solution.py:88
  818.6 71.0 %while.62 = (s32[]{:T(128)}, f32[8,256]{1,0:T(8,128)S(1)}, f32[8,6,256]{2,1,0:T(8,128)S(1)}, f32[8]{0:T(128)S(1)}, bf16[8,256,128]{2,1,0:T(8,128)(2,1)S(1)}, /*i...) while((s32[]{:T(128)}, f32[8,256]{1,0:T(8,128)S(1)}, ...), condition=%wide.region_24.26_spmd, body=%wide.region_22.25_spmd.sunk | while | flops 234756352 | bytes 9386733 | solution.py:90
  893.1 62.3 %psum.91 = f32[1,256]{1,0:T(1,128)S(1)} all-reduce(f32[1,256]{1,0:T(1,128)S(1)} %fusion.163), channel_id=1, replica_groups=mesh['grp'=8,'leaf'=32] {'leaf'}, use_global_device_ids=true, to_apply=%region_26.28 | all-reduce | flops 256 | bytes 2048 | tf_op jit(solution)/shard_map/psum | solution.py:109
  955.4 11.1 all-gather.2
  973.0 77.1 %psum.92 = f32[]{:T(128)} all-reduce(f32[]{:T(128)} %multiply_reduce_fusion.3), channel_id=1, replica_groups=mesh['grp'=8,'leaf'=32] {'grp','leaf'}, use_global_device_ids=true, to_apply=%region_28.30 | all-reduce | flops 1 | bytes 8 | tf_op jit(solution)/shard_map/psum | solution.py:82
  1052.0 74.3 %psum.93 = f32[]{:T(128)} all-reduce(f32[]{:T(128)} %get-tuple-element.643), channel_id=1, replica_groups=mesh['grp'=8,'leaf'=32] {'grp','leaf'}, use_global_device_ids=true, to_apply=%region_30.32 | all-reduce | flops 1 | bytes 8 | tf_op jit(solution)/shard_map/psum | solution.py:82
  1127.7 25.1 %all_gather.38 = f32[65536]{0:T(1024)S(1)} all-gather(f32[2048]{0:T(1024)S(1)} %multiply_add_fusion.6), channel_id=1, replica_groups=mesh['grp'=8,'leaf'=32] {'leaf'}, dimensions={0}, use_global_device_ids=true | all-gather | bytes 270336 | tf_op jit(solution)/shard_map/all_gather | solution.py:88
  1153.6 70.9 %while.63 = (s32[]{:T(128)}, f32[8,256]{1,0:T(8,128)S(1)}, f32[8,6,256]{2,1,0:T(8,128)S(1)}, f32[8]{0:T(128)S(1)}, bf16[8,256,128]{2,1,0:T(8,128)(2,1)S(1)}, /*i...) while((s32[]{:T(128)}, f32[8,256]{1,0:T(8,128)S(1)}, ...), condition=%wide.region_33.35_spmd, body=%wide.region_31.34_spmd.sunk | while | flops 234756352 | bytes 9386733 | solution.py:90
  1228.0 62.4 %psum.94 = f32[1,256]{1,0:T(1,128)S(1)} all-reduce(f32[1,256]{1,0:T(1,128)S(1)} %fusion.165), channel_id=1, replica_groups=mesh['grp'=8,'leaf'=32] {'leaf'}, use_global_device_ids=true, to_apply=%region_35.37 | all-reduce | flops 256 | bytes 2048 | tf_op jit(solution)/shard_map/psum | solution.py:109
  1307.7 77.3 %psum.95 = f32[]{:T(128)} all-reduce(f32[]{:T(128)} %multiply_reduce_fusion.1), channel_id=1, replica_groups=mesh['grp'=8,'leaf'=32] {'grp','leaf'}, use_global_device_ids=true, to_apply=%region_37.39 | all-reduce | flops 1 | bytes 8 | tf_op jit(solution)/shard_map/psum | solution.py:82
  (584 shorter events, 373.1 us)
Async XLA Ops:
  7.2 8.9 copy-start
  7.2 92.9 %all-gather.6.cloned.1.call-start = ((), (), s32[]{:S(2)}) async-start(), calls=%async_computation.4 | async-start | bytes 17301504 | tf_op jit(solution)/shard_map/all_gather | solution.py:61
  9.9 6.2 copy-start.11
  9.9 6.2 copy-start.12
  16.8 1.3 copy-start.8
  16.8 1.4 copy-start.6
  16.8 1.4 copy-start.7
  16.8 1.5 copy-start.9
  16.9 28.7 %copy-start.10 = (s32[1,256]{1,0:T(1,128)S(1)}, s32[1,256]{1,0:T(1,128)}, u32[]{:S(2)}) copy-start(s32[1,256]{1,0:T(1,128)} %param.29) | copy-start | bytes 3076
  18.0 90.8 %copy-start.5 = (bf16[2048,128]{1,0:T(8,128)(2,1)S(1)}, bf16[2048,128]{1,0:T(8,128)(2,1)}, u32[]{:S(2)}) copy-start(bf16[2048,128]{1,0:T(8,128)(2,1)} %multiply_convert_fusion) | copy-start | bytes 1572868
  18.0 285.5 %reduce-scatter.5.cloned.1.call-start = ((), (), s32[]{:S(2)}) async-start(), calls=%async_computation.5 | async-start | bytes 135168 | tf_op jit(solution)/shard_map/reduce_scatter | solution.py:102
  215.0 2.8 copy-start.1
  215.9 420.2 %reduce-scatter.7.cloned.1.call-start = ((), (), s32[]{:S(2)}) async-start(), calls=%async_computation.6 | async-start | bytes 135168 | tf_op jit(solution)/shard_map/reduce_scatter | solution.py:102
  555.2 416.5 %reduce-scatter.9.cloned.1.call-start = ((), (), s32[]{:S(2)}) async-start(), calls=%async_computation.7 | async-start | bytes 135168 | tf_op jit(solution)/shard_map/reduce_scatter | solution.py:102
  557.8 76.5 %copy-start.2 = (f32[2048,256]{1,0:T(8,128)S(1)}, f32[2048,256]{1,0:T(8,128)}, u32[]{:S(2)}) copy-start(f32[2048,256]{1,0:T(8,128)} %fusion.135) | copy-start | bytes 6291460
  890.5 415.8 %reduce-scatter.11.cloned.1.call-start = ((), (), s32[]{:S(2)}) async-start(), calls=%async_computation.8 | async-start | bytes 135168 | tf_op jit(solution)/shard_map/reduce_scatter | solution.py:102
  893.1 76.7 %copy-start.3 = (f32[2048,256]{1,0:T(8,128)S(1)}, f32[2048,256]{1,0:T(8,128)}, u32[]{:S(2)}) copy-start(f32[2048,256]{1,0:T(8,128)} %fusion.135) | copy-start | bytes 6291460
  1228.0 76.5 %copy-start.4 = (f32[2048,256]{1,0:T(8,128)S(1)}, f32[2048,256]{1,0:T(8,128)}, u32[]{:S(2)}) copy-start(f32[2048,256]{1,0:T(8,128)} %fusion.135) | copy-start | bytes 6291460
Sparse Core Ops, SparseCore 0:
  18.2 81.8 all-gather.5
  216.1 82.3 reduce-scatter.4
  555.3 74.4 reduce-scatter.6
  890.7 74.2 reduce-scatter.8
  1225.6 74.3 reduce-scatter.10
where the time goes:
time: 1400 us; the launch traced here: 1390 us
  blocking collectives  952 us (68%)
  matrix products  271 us (19%)
  waiting for transfers between devices  54.3 us (4%)
  local copies, waits for them, and re-layouts  50.2 us (4%)
  other arithmetic  40.6 us (3%)
  between operations  23.8 us (2%)
    psum x7, blocking collectives, inner_total(): return lax.psum(jnp.sum(left * right), ('grp', 'leaf'))  530 us
    psum x4, blocking collectives, on_device(): group_total = lax.psum(apply_local_charge, 'leaf')  255 us
    all_gather x4, blocking collectives, on_device(): whole = lax.all_gather(direction, 'leaf', axis=0, tiled=True)  102 us
    all_gather x1, waiting for transfers between devices, on_device(): group_feat = lax.all_gather(own_features, 'leaf', axis=0, tiled=True)  54.2 us
    dot_general x32, matrix products, near_tiles(): jnp.einsum('kij,kj->ki', partner_tile, part_vec, precision=highest)  51.6 us
    dot_general x32, matrix products, near_tiles(): jnp.einsum('kif,kjf->kij', part_feat, part_feat, preferred_element_type=j...  47.5 us
    dot_general x32, matrix products, near_tiles(): jnp.einsum('kij,i->kj', cross, own_vec, precision=highest)  46.2 us
    dot_general x32, matrix products, near_tiles(): jnp.einsum('if,kjf->kij', own_feat, part_feat, preferred_element_type=jnp...  44.1 us
  transfers between devices with their start and end apart: 5, of which 1 were waited for; matrix products, arithmetic and copies ran while one was open for 2% of the time, Pallas kernels for 0%

commit v1 on v0

v1 whole, which is shorter than its diff:
```python
import jax
import jax.numpy as jnp
from jax import lax
from jax.experimental import pallas as pl
from jax.experimental.pallas import tpu as pltpu
from jax.sharding import PartitionSpec as P

BLK = 256
NEAR = 6
ITERS = 4
N_GRP = 8
N_LEAF = 32
OWN = 8
ROWS_DEV = OWN * BLK
HALF = BLK // 2
F32 = jnp.float32
BF16 = jnp.bfloat16
MESH = pl.DeviceIdType.MESH
SHARP = 10.0 * 1.4426950408889634


def mm(left, right):
    return lax.dot_general(left, right, (((1,), (0,)), ((), ())), preferred_element_type=F32)


def mm_t(left, right):
    return lax.dot_general(left, right, (((1,), (1,)), ((), ())), preferred_element_type=F32)


def iota(shape, dim):
    return lax.broadcasted_iota(jnp.int32, shape, dim)


def kernel_of(inner):
    return jnp.exp2(inner * SHARP - SHARP)


def unit(raw):
    return (raw * lax.rsqrt(jnp.sum(raw * raw, -1, keepdims=True) + 1e-06)).astype(BF16)


def split2(values):
    high = values.astype(BF16).astype(F32)
    return high, (values - high).astype(BF16).astype(F32)


def rows16(values):
    return jnp.concatenate(split2(values), 0).astype(BF16)


def spread(values):
    wide = jnp.concatenate([jnp.concatenate(split2(values), 0)] * OWN, 1)
    shape = (16, ROWS_DEV)
    keep = (iota(shape, 0) & 7) == (iota(shape, 1) >> 8)
    return jnp.where(keep, wide, 0.0).astype(BF16)


def own_part(wide):
    both = wide[:8] + wide[8:]
    row = iota((8, BLK), 0)
    total = jnp.zeros((8, BLK), F32)
    for n in range(OWN):
        total = total + jnp.where(row == n, both[:, n * BLK : (n + 1) * BLK], 0.0)
    return total


def halves(values):
    return jnp.concatenate([values[:8], values[8:]], 1)


def sum_all(values):
    folded = values[:, :128] + values[:, 128:]
    return jnp.broadcast_to(jnp.sum(folded, (0, 1), keepdims=True), (8, 128))


def wide(values):
    return jnp.concatenate([values, values], 1)


def column_of(row):
    return jnp.transpose(jnp.broadcast_to(row.astype(F32), (128, 128)))


def body(
    cfg_ref, order_ref, w_in_ref, bias_ref, w_out_ref, noise_ref, rhs_ref, nb_ref, live_ref, skel_ref,
    nb_s, skel_s,
    x_out, r_out,
    grp_cfg, tiles, coup, skel_all, slabs, pick, pick_t,
    msg_a, ret_send, ret_recv, quad, grp_q, grp_s,
    g_send, g_recv, s_send, s_recv, k_sem, it_sem,
):
    grp = lax.axis_index("grp")
    me = lax.axis_index("leaf")
    core = lax.rem(me, 2)
    xx = lax.rem(me // 2, 4)
    yy = me // 8

    def leaf_at(y, x, c):
        return lax.rem(y + 4, 4) * 8 + lax.rem(x + 4, 4) * 2 + c

    def leaf_peer(j):
        return lax.rem(me + j, N_LEAF)

    def grp_peer(j):
        return lax.rem(grp + j, N_GRP)

    barrier = pltpu.get_barrier_semaphore()

    def greet_leaf(j, _):
        pl.semaphore_signal(barrier, inc=1, device_id=(grp, leaf_peer(j)), device_id_type=MESH)
        return 0

    def greet_grp(j, _):
        pl.semaphore_signal(barrier, inc=1, device_id=(grp_peer(j), me), device_id_type=MESH)
        return 0

    lax.fori_loop(1, N_LEAF, greet_leaf, 0)
    lax.fori_loop(1, N_GRP, greet_grp, 0)

    spot0 = (iota((64, 128), 0) == iota((64, 128), 1)).astype(F32).astype(BF16)
    spot1 = (iota((64, 128), 0) + 64 == iota((64, 128), 1)).astype(F32).astype(BF16)
    lane = iota((128, 128), 1).astype(F32)

    def permute(b, _):
        packed = jnp.zeros((HALF, 128), F32)
        for half, spot in ((0, spot0), (1, spot1)):
            column = column_of(order_ref[pl.ds(2 * b + half, 1), :])
            chosen = jnp.concatenate(
                [jnp.where(column == lane + 128.0 * t, 1.0, 0.0).astype(BF16) for t in range(ROWS_DEV // 128)], 1
            )
            packed = packed + mm(mm(chosen, cfg_ref[...]).astype(BF16), spot)
        grp_cfg[me * OWN + b] = packed.astype(BF16)
        return 0

    lax.fori_loop(0, OWN, permute, 0)
    pl.semaphore_wait(barrier, N_LEAF - 1 + N_GRP - 1)

    def at(half, first, second):
        return leaf_at(yy + second, xx + first, core) if half == 0 else leaf_at(yy + first, xx + second, core)

    def piece(leaf, half, quarter=None):
        if quarter is None:
            return grp_cfg.at[pl.ds(leaf * OWN + 4 * half, 4)]
        return grp_cfg.at[pl.ds(leaf * OWN + 4 * half + 2 * quarter, 2)]

    def hop(half, index, ref, target):
        return pltpu.make_async_remote_copy(
            src_ref=ref, dst_ref=ref, send_sem=g_send.at[half, index], recv_sem=g_recv.at[half, index],
            device_id=(grp, target), device_id_type=MESH,
        )

    sibling = me - core + lax.rem(core + 1, 2)

    def to_sibling(half, index, leaf):
        ref = piece(leaf, half)
        copy = pltpu.make_async_remote_copy(
            src_ref=ref, dst_ref=ref, send_sem=s_send.at[half, index], recv_sem=s_recv.at[half, index],
            device_id=(grp, sibling), device_id_type=MESH,
        )
        copy.start()
        return copy

    started = []

    def start(copy):
        copy.start()
        started.append(copy)

    offsets = (0, -1, 1, 2)

    def second_axis(half, p):
        ref = piece(at(half, offsets[p], 0), half)
        start(hop(half, 4 + 4 * p, ref, at(half, 0, 1)))
        start(hop(half, 5 + 4 * p, ref, at(half, 0, -1)))
        started.append(to_sibling(half, 4 * p, at(half, offsets[p], 0)))

    def arrived(half, index, ref):
        hop(half, index, ref, me).wait_recv()

    for half in range(2):
        own = piece(me, half)
        start(hop(half, 0, own, at(half, 1, 0)))
        start(hop(half, 1, own, at(half, -1, 0)))
    for half in range(2):
        second_axis(half, 0)
    for half in range(2):
        left, right = at(half, -1, 0), at(half, 1, 0)
        arrived(half, 0, piece(left, half))
        start(hop(half, 2, piece(left, half, 0), right))
        arrived(half, 1, piece(right, half))
        start(hop(half, 3, piece(right, half, 1), left))
    for half in range(2):
        second_axis(half, 1)
        second_axis(half, 2)
    for p in range(4):
        for half in range(2):
            if p == 1:
                far = at(half, 2, 0)
                arrived(half, 2, piece(far, half, 0))
                arrived(half, 3, piece(far, half, 1))
                second_axis(half, 3)
        for half in range(2):
            down, up = at(half, offsets[p], -1), at(half, offsets[p], 1)
            arrived(half, 4 + 4 * p, piece(down, half))
            start(hop(half, 6 + 4 * p, piece(down, half, 0), at(half, 0, 1)))
            started.append(to_sibling(half, 4 * p + 1, down))
            arrived(half, 5 + 4 * p, piece(up, half))
            start(hop(half, 7 + 4 * p, piece(up, half, 1), at(half, 0, -1)))
            started.append(to_sibling(half, 4 * p + 2, up))
        for half in range(2):
            over = at(half, offsets[p], 2)
            arrived(half, 6 + 4 * p, piece(over, half, 0))
            arrived(half, 7 + 4 * p, piece(over, half, 1))
            started.append(to_sibling(half, 4 * p + 3, over))
    steps = (0, -1, 1, 2)
    for p in range(4):
        for half in range(2):
            for s in range(4):
                theirs = at(half, offsets[p], steps[s]) - core + lax.rem(core + 1, 2)
                ref = piece(theirs, half)
                pltpu.make_async_remote_copy(
                    src_ref=ref, dst_ref=ref, send_sem=s_send.at[half, 4 * p + s], recv_sem=s_recv.at[half, 4 * p + s],
                    device_id=(grp, sibling), device_id_type=MESH,
                ).wait_recv()
    for copy in started:
        copy.wait_send()

    w_in = w_in_ref[...]
    none = jnp.zeros_like(w_in)
    w_pair = jnp.concatenate([jnp.concatenate([w_in, none], 1), jnp.concatenate([none, w_in], 1)], 0)
    bias = jnp.concatenate([bias_ref[...], bias_ref[...]], 1)
    w_out = w_out_ref[...]

    def hidden_of(packed):
        return jnp.tanh(mm(packed, w_pair) + bias)

    def slab(r, _):
        block = grp_cfg[skel_s[0, r]].astype(F32)
        kept = jnp.where(iota((HALF, 128), 0) >> 4 == jnp.broadcast_to(skel_s[1, r], (HALF, 128)), block, 0.0)
        slabs[r] = jnp.sum(kept.reshape(8, 16, 128), 0).astype(BF16)
        return 0

    lax.fori_loop(0, BLK, slab, 0)
    every = slabs[...].reshape(BLK * 16, 128)
    for part in range(2):
        column = jnp.transpose(jnp.broadcast_to(skel_ref[pl.ds(part, 1), :], (128, 128)).astype(F32)).astype(jnp.int32)
        aim = (column & 15) + 16 * iota((128, 128), 0)
        chosen = jnp.concatenate(
            [jnp.where(aim == iota((128, 128), 1) + 128 * t, 1.0, 0.0).astype(BF16) for t in range(16)], 1
        )
        packed = mm(chosen, every[part * 2048 : (part + 1) * 2048]).astype(BF16)
        hidden = hidden_of(packed)
        hidden = jnp.where((column & HALF) != 0, hidden[:, 128:], hidden[:, :128]).astype(BF16)
        skel_all[grp, pl.ds(part * 128, 128), :] = unit(mm(hidden, w_out))

    def skel_copy(j):
        return pltpu.make_async_remote_copy(
            src_ref=skel_all.at[grp], dst_ref=skel_all.at[grp], send_sem=k_sem.at[0], recv_sem=k_sem.at[1],
            device_id=(grp_peer(j), me), device_id_type=MESH,
        )

    def start_skel(j, _):
        skel_copy(j).start()
        return 0

    lax.fori_loop(1, N_GRP, start_skel, 0)

    skel_feat = skel_all[grp]

    def tile_row(n, _):
        packed = jnp.concatenate(
            [grp_cfg[nb_s[n, k]] for k in range(NEAR)] + [grp_cfg[me * OWN + n]], 0
        )
        hidden = hidden_of(packed).astype(BF16)
        feats = [unit(mm(hidden[:, :128], w_out)), unit(mm(hidden[:, 128:], w_out))]
        own = jnp.concatenate([f[NEAR * HALF :] for f in feats], 0)
        rows = pl.ds(n * BLK, BLK)
        for h in range(2):
            made = kernel_of(mm_t(own, feats[h])).astype(BF16)
            for k in range(NEAR):
                tiles[k, rows, h * 128 : (h + 1) * 128] = made[:, k * 128 : (k + 1) * 128]
            tiles[NEAR + 1, rows, h * 128 : (h + 1) * 128] = made[:, NEAR * 128 :]
        tiles[NEAR, rows, :] = kernel_of(mm_t(own, skel_feat)).astype(BF16)
        return 0

    lax.fori_loop(0, OWN, tile_row, 0)

    nb = nb_ref[...]
    live = live_ref[...].astype(F32)
    place = nb + (nb & -8)
    for h in range(2):
        for k in range(NEAR):
            hit = iota((8, 512), 1) == place[:, k : k + 1] + 8 * h
            pick[pl.ds((h * NEAR + k) * 8, 8), :] = jnp.where(hit, live[:, k : k + 1], 0.0)
    pick[pl.ds(96, 32), :] = jnp.zeros((32, 512), F32)
    for q in range(4):
        pick_t[pl.ds(q * 128, 128), :] = jnp.transpose(pick[:, q * 128 : (q + 1) * 128]).astype(BF16)
    count = jnp.zeros((8, BLK), F32)
    for k in range(NEAR):
        count = count + jnp.where(iota((8, BLK), 1) == nb[:, k : k + 1], live[:, k : k + 1], 0.0)
    count = jnp.sum(count, 0, keepdims=True)
    own_uses = jnp.sum(live, 1, keepdims=True)

    many = skel_all.at[pl.ds(0, N_GRP - 1)]
    pltpu.make_async_copy(many, many, k_sem.at[1]).wait()
    pltpu.make_async_copy(many, many, k_sem.at[0]).wait()

    def couple(g, _):
        coup[pl.ds(g * BLK, BLK), :] = kernel_of(mm_t(skel_all[g], skel_feat)).astype(BF16)
        return 0

    lax.fori_loop(0, N_GRP, couple, 0)

    noise = jnp.concatenate([noise_ref[pl.ds(0, 8, stride=2), :], noise_ref[pl.ds(1, 8, stride=2), :]], 1)
    right = jnp.concatenate([rhs_ref[pl.ds(0, 8, stride=2), :], rhs_ref[pl.ds(1, 8, stride=2), :]], 1)
    precond = 1.0 / (1.0 + noise)
    zero = jnp.zeros((8, BLK), F32)
    one = jnp.ones((8, 128), F32)

    def iteration(t, carry):
        x, r, direction, image, gamma_old, energy_old = carry
        sem = it_sem.at[t]
        u = r * precond
        gamma_own = sum_all(r * u)
        mixed_own = sum_all(u * image)
        u_wide = spread(u)
        charge = jnp.sum(mm(u_wide, tiles[NEAR]), 0, keepdims=True)

        c_high, c_mid = split2(charge)
        g_high, g_mid = split2(gamma_own)
        g_low = gamma_own - g_high - g_mid
        m_high, m_mid = split2(mixed_own)
        m_low = mixed_own - m_high - m_mid
        row = iota((16, 128), 0)
        extra = jnp.zeros((16, 128), F32)
        for at_row, values in enumerate(
            (c_high[:, :128], c_high[:, 128:], c_mid[:, :128], c_mid[:, 128:], count[:, :128], count[:, 128:],
             g_high[:1], g_mid[:1], g_low[:1], m_high[:1], m_mid[:1], m_low[:1])
        ):
            extra = jnp.where(row == at_row, values, extra)
        msg_a[t, me, pl.ds(0, 16), :] = jnp.concatenate([u[:, :128], u[:, 128:]], 0).astype(BF16)
        msg_a[t, me, pl.ds(16, 16), :] = extra.astype(BF16)

        def send_a(j, _):
            pltpu.make_async_remote_copy(
                src_ref=msg_a.at[t, me], dst_ref=msg_a.at[t, me], send_sem=sem.at[0], recv_sem=sem.at[1],
                device_id=(grp, leaf_peer(j)), device_id_type=MESH,
            ).start()
            return 0

        lax.fori_loop(1, N_LEAF, send_a, 0)

        backs = []
        for k in range(NEAR):
            made = mm(u_wide, tiles[k])
            backs.append(made[:8] + made[8:])
        stack = jnp.concatenate([b[:, :128] for b in backs] + [b[:, 128:] for b in backs] + [jnp.zeros((32, 128), F32)], 0)
        b_high, b_mid = split2(stack)
        returned = mm(pick_t[...], b_high.astype(BF16)) + mm(pick_t[...], b_mid.astype(BF16))
        ret_send[t] = returned.reshape(N_LEAF, 16, 128).astype(BF16)
        ret_recv[t, me] = ret_send[t, me]

        def send_r(j, _):
            peer = leaf_peer(j)
            pltpu.make_async_remote_copy(
                src_ref=ret_send.at[t, peer], dst_ref=ret_recv.at[t, me], send_sem=sem.at[2], recv_sem=sem.at[3],
                device_id=(grp, peer), device_id_type=MESH,
            ).start()
            return 0

        lax.fori_loop(1, N_LEAF, send_r, 0)
        made = mm(u_wide, tiles[NEAR + 1])
        self_part = made[:8] + made[8:]

        many = msg_a.at[t, pl.ds(0, N_LEAF - 1)]
        pltpu.make_async_copy(many, many, sem.at[1]).wait()
        extra = jnp.sum(msg_a[t, :, pl.ds(16, 16), :].astype(F32), 0)
        charge = jnp.concatenate([extra[0:1] + extra[2:3], extra[1:2] + extra[3:4]], 1)
        counts = jnp.broadcast_to(jnp.concatenate([extra[4:5], extra[5:6]], 1), (8, BLK))
        mine = iota((8, BLK), 1) == me * OWN + iota((8, BLK), 0)
        weight = own_uses + jnp.sum(jnp.where(mine, counts, 0.0), 1, keepdims=True)
        self_part = weight * self_part
        row = iota((8, 128), 0)
        tile = jnp.where(row == 0, charge[:, :128], 0.0)
        tile = jnp.where(row == 1, charge[:, 128:], tile)
        tile = jnp.where(row == 2, extra[6:7] + extra[7:8] + extra[8:9], tile)
        tile = jnp.where(row == 3, extra[9:10] + extra[10:11] + extra[11:12], tile)
        grp_q[t, grp] = tile

        def send_q(j, _):
            pltpu.make_async_remote_copy(
                src_ref=grp_q.at[t, grp], dst_ref=grp_q.at[t, grp], send_sem=sem.at[4], recv_sem=sem.at[5],
                device_id=(grp_peer(j), me), device_id_type=MESH,
            ).start()
            return 0

        lax.fori_loop(1, N_GRP, send_q, 0)

        vectors = msg_a[t, :, pl.ds(0, 16), :].reshape(N_LEAF * 16, 128)
        found = mm(pick[...].astype(BF16), vectors)
        partners = [
            jnp.concatenate([found[k * 8 : k * 8 + 8], found[(NEAR + k) * 8 : (NEAR + k) * 8 + 8]], 1) for k in range(NEAR)
        ]
        share = u * (self_part + noise * u)
        for k in range(NEAR):
            share = share + 2.0 * backs[k] * partners[k]
        quad[t, me] = sum_all(share)[:1]

        def send_s(j, _):
            pltpu.make_async_remote_copy(
                src_ref=quad.at[t, me], dst_ref=quad.at[t, me], send_sem=sem.at[6], recv_sem=sem.at[7],
                device_id=(grp, leaf_peer(j)), device_id_type=MESH,
            ).start()
            return 0

        lax.fori_loop(1, N_LEAF, send_s, 0)

        forward = jnp.zeros((16, ROWS_DEV), F32)
        for k in range(NEAR):
            forward = forward + mm_t(jnp.concatenate([partners[k], zero], 0).astype(BF16), tiles[k])
        near = self_part + own_part(forward)

        many = grp_q.at[t, pl.ds(0, N_GRP - 1)]
        pltpu.make_async_copy(many, many, sem.at[5]).wait()
        row = iota((8, BLK), 0)
        charges = zero
        sums = jnp.zeros((8, 128), F32)
        for g in range(N_GRP):
            tile = grp_q[t, g]
            charges = jnp.where(row == g, jnp.concatenate([tile[0:1], tile[1:2]], 1), charges)
            sums = sums + tile
        gamma = jnp.broadcast_to(sums[2:3], (8, 128))
        mixed = jnp.broadcast_to(sums[3:4], (8, 128))
        field = jnp.sum(mm(spread(charges), coup[...]), 0, keepdims=True)
        far_share = sum_all(jnp.where(row == 0, charge * field, 0.0))
        many = quad.at[t, pl.ds(0, N_LEAF - 1)]
        pltpu.make_async_copy(many, many, sem.at[7]).wait()
        grp_s[t, grp] = jnp.sum(quad[t], 0) + far_share[:1]

        def send_c(j, _):
            pltpu.make_async_remote_copy(
                src_ref=grp_s.at[t, grp], dst_ref=grp_s.at[t, grp], send_sem=sem.at[8], recv_sem=sem.at[9],
                device_id=(grp_peer(j), me), device_id_type=MESH,
            ).start()
            return 0

        lax.fori_loop(1, N_GRP, send_c, 0)
        far = own_part(mm_t(rows16(jnp.broadcast_to(field, (8, BLK))), tiles[NEAR]))
        many = ret_recv.at[t, pl.ds(0, N_LEAF - 1)]
        pltpu.make_async_copy(many, many, sem.at[3]).wait()
        near = near + halves(jnp.sum(ret_recv[t].astype(F32), 0))
        applied = near + far + noise * u

        many = grp_s.at[t, pl.ds(0, N_GRP - 1)]
        pltpu.make_async_copy(many, many, sem.at[9]).wait()
        quadratic = jnp.broadcast_to(jnp.sum(grp_s[t], 0), (8, 128))
        beta = jnp.where(t == 0, jnp.zeros_like(gamma), gamma / gamma_old)
        energy = quadratic + 2.0 * beta * mixed + beta * beta * energy_old
        alpha = wide(gamma / energy)
        direction = u + wide(beta) * direction
        image = applied + wide(beta) * image
        x = x + alpha * direction
        r = r - alpha * image

        for index, sent in (
            (0, msg_a.at[t, pl.ds(0, N_LEAF - 1)]),
            (2, ret_recv.at[t, pl.ds(0, N_LEAF - 1)]),
            (4, grp_q.at[t, pl.ds(0, N_GRP - 1)]),
            (6, quad.at[t, pl.ds(0, N_LEAF - 1)]),
            (8, grp_s.at[t, pl.ds(0, N_GRP - 1)]),
        ):
            pltpu.make_async_copy(sent, sent, sem.at[index]).wait()
        return x, r, direction, image, gamma, energy

    x, r, *_ = lax.fori_loop(0, ITERS, iteration, (zero, right, zero, zero, one, one))
    for ref, values in ((x_out, x), (r_out, r)):
        ref[pl.ds(0, 8, stride=2), :] = values[:, :128]
        ref[pl.ds(1, 8, stride=2), :] = values[:, 128:]


def on_device(
    configs, order, w_in, bias_in, w_out, noise, right_side, near_blocks, near_live, skeleton
):
    vmem = pl.BlockSpec(memory_space=pltpu.VMEM)
    smem = pl.BlockSpec(memory_space=pltpu.SMEM)
    dma = pltpu.SemaphoreType.DMA
    solution_, residual_ = pl.pallas_call(
        body,
        out_shape=[jax.ShapeDtypeStruct((16, 128), F32)] * 2,
        in_specs=[vmem] * 10 + [smem] * 2,
        out_specs=[vmem] * 2,
        scratch_shapes=[
            pltpu.VMEM((N_LEAF * OWN, HALF, 128), BF16),
            pltpu.VMEM((NEAR + 2, ROWS_DEV, BLK), BF16),
            pltpu.VMEM((N_GRP * BLK, BLK), BF16),
            pltpu.VMEM((N_GRP, BLK, 128), BF16),
            pltpu.VMEM((BLK, 16, 128), BF16),
            pltpu.VMEM((128, 512), F32),
            pltpu.VMEM((512, 128), BF16),
            pltpu.VMEM((ITERS, N_LEAF, 32, 128), BF16),
            pltpu.VMEM((ITERS, N_LEAF, 16, 128), BF16),
            pltpu.VMEM((ITERS, N_LEAF, 16, 128), BF16),
            pltpu.VMEM((ITERS, N_LEAF, 1, 128), F32),
            pltpu.VMEM((ITERS, N_GRP, 8, 128), F32),
            pltpu.VMEM((ITERS, N_GRP, 1, 128), F32),
            dma((2, 20)),
            dma((2, 20)),
            dma((2, 16)),
            dma((2, 16)),
            dma((2,)),
            dma((ITERS, 10)),
        ],
        compiler_params=pltpu.CompilerParams(
            collective_id=0, has_side_effects=True, vmem_limit_bytes=56 * 2**20
        ),
        cost_estimate=pl.CostEstimate(flops=10**10, bytes_accessed=10**7, transcendentals=10**7),
    )(
        configs, order.reshape(16, 128), w_in, bias_in.reshape(1, 128), w_out,
        noise.reshape(16, 128), right_side.reshape(16, 128), near_blocks, near_live, skeleton.reshape(2, 128),
        near_blocks, jnp.concatenate([skeleton // BLK, skeleton % HALF // 16], 0),
    )
    return solution_.reshape(-1), residual_.reshape(-1)


def solution(mesh):
    in_specs = (
        P(("grp", "leaf"), None),
        P(("grp", "leaf"), None),
        P(),
        P(),
        P(),
        P(("grp", "leaf")),
        P(("grp", "leaf")),
        P(("grp", "leaf"), None),
        P(("grp", "leaf"), None),
        P("grp", None),
    )
    out_specs = (P(("grp", "leaf")), P(("grp", "leaf")))
    return jax.shard_map(
        on_device, mesh=mesh, in_specs=in_specs, out_specs=out_specs, check_vma=False
    )
```

time: 1400 us -> 142 us (0.10)
  blocking collectives: 952 us -> 0 us
  matrix products: 271 us -> 0 us
  Pallas kernels: 0 us -> 137 us
  waiting for transfers between devices: 54.3 us -> 0 us
  local copies, waits for them, and re-layouts: 50.2 us -> 4.53 us
  other arithmetic: 40.6 us -> 0.6 us
  between operations: 23.8 us -> 0.66 us
    psum x11 -> x0, blocking collectives: 785 us -> none  [the longest x7 530 us: inner_total(): return lax.psum(jnp.sum(left * right), ('grp', 'leaf'))]
    dot_general x243 -> x0, matrix products: 271 us -> none  [the longest x32 51.6 us: near_tiles(): jnp.einsum('kij,kj->ki', partner_tile, part_vec, precision=highest)]
    all_gather x9 -> x0, blocking collectives: 167 us -> none  [the longest x4 102 us: on_device(): whole = lax.all_gather(direction, 'leaf', axis=0, tiled=True)]
    pallas_call x0 -> x1, Pallas kernels: none -> 137 us  [on_device(): pl.pallas_call(body, out_shape=[jax.ShapeDtypeStruct((16, 128), F32)] * 2...]
    all_gather x1 -> x0, waiting for transfers between devices: 54.2 us -> none  [on_device(): group_feat = lax.all_gather(own_features, 'leaf', axis=0, tiled=True)]
    gather x11 -> x0, local copies, waits for them, and re-layouts: 25.9 us -> none  [the longest x1 8.65 us: on_device(): skel_feat = jnp.take(group_feat, skeleton[0], axis=0)]
    add x35 -> x0, other arithmetic: 20.8 us -> none  [the longest x32 20.7 us: near_tiles(): own_out + jnp.sum(weights[:, None] * jnp.einsum('kij,kj->ki', cross, part...]
    dynamic_slice x32 -> x0, local copies, waits for them, and re-layouts: 20.5 us -> none  [on_device(): lax.map(near_tiles, (own_blocks, part_feat, direction.reshape(blocks_dev,...]
  transfers between devices with their start and end apart: 5 -> 0, of which waited for: 1 -> 0; matrix products, arithmetic and copies ran while one was open for 2% -> 0% of each run, Pallas kernels for 0% -> 0%
where the time goes in v1:
time: 142 us
  Pallas kernels  137 us (96%)
  local copies, waits for them, and re-layouts  4.53 us (3%)
    pallas_call x1, Pallas kernels, on_device(): pl.pallas_call(body, out_shape=[jax.ShapeDtypeStruct((16, 128), F32)] * 2...  137 us
    unnamed x7, local copies, waits for them, and re-layouts  4.53 us

profile of v1, /device:TPU:1, one launch (start us, length us, event | category | flops | bytes accessed | tf_op | source)
XLA Modules:
  0.0 142.3 jit_solution(16699780518606871038)
XLA Ops:
  0.6 0.0 copy-start.1
  0.6 0.7 copy-done.1
  1.3 0.6 pad_add_fusion.skel_s
  1.9 1.9 %copy.12.cfg_ref = bf16[2048,64]{1,0:T(8,128)(2,1)} copy(bf16[2048,64]{0,1:T(8,128)(2,1)} %param.10) | data formatting | bytes 524288 | tf_op args[0]
  3.9 136.5 %shard_map.113 = (f32[16,128]{1,0:T(8,128)}, f32[16,128]{1,0:T(8,128)}) custom-call(bf16[2048,64]{1,0:T(8,128)(2,1)} %copy.12.cfg_ref, s32[16,128]{1,0:T(8,128)} %bitcast.10, bf16[64,128]{1,0:T(8,128)(2,1)} %w_in_ref.1, f32[1,128]{1,0:T(1,128)} %bitcast.13, bf16[128,128]{1,0:T(8,128)(2,1)} %w_out_ref.1, f32[16,128]{1,0:T(8,128)} %bitcast.11, ...), custom_call_target="tpu_custom_call" | custom-call | flops 10000000000 | bytes 10000000 | tf_op jit(solution)/shard_map/pallas_call | solution.py:487
  140.4 0.0 copy-start
  140.4 1.3 copy.15
  141.7 0.0 copy-done
  141.7 0.6 copy.16
  (1 shorter events, 0.0 us)
Async XLA Ops:
  0.6 0.7 copy-start.1
  140.4 1.3 copy-start

commit v2 on v1

v2 whole, which is shorter than its diff:
```python
import jax
import jax.numpy as jnp
from jax import lax
from jax.experimental import pallas as pl
from jax.experimental.pallas import tpu as pltpu
from jax.sharding import PartitionSpec as P

BLK = 256
NEAR = 6
ITERS = 4
N_GRP = 8
N_LEAF = 32
OWN = 8
ROWS_DEV = OWN * BLK
F32 = jnp.float32
BF16 = jnp.bfloat16
MESH = pl.DeviceIdType.MESH
SHARP = 10.0 * 1.4426950408889634


def mm(left, right):
    return lax.dot_general(left, right, (((1,), (0,)), ((), ())), preferred_element_type=F32)


def mm_t(left, right):
    return lax.dot_general(left, right, (((1,), (1,)), ((), ())), preferred_element_type=F32)


def iota(shape, dim):
    return lax.broadcasted_iota(jnp.int32, shape, dim)


def kernel_of(inner):
    return jnp.exp2(inner * SHARP - SHARP)


def one_hot(row, base):
    hit = jnp.broadcast_to(row, (BLK, BLK)) == iota((BLK, BLK), 0) + base
    return jnp.where(hit, 1.0, 0.0).astype(BF16)


def flip(values):
    return jnp.transpose(values.astype(F32)).astype(BF16)


def split2(values):
    high = values.astype(BF16).astype(F32)
    return high, (values - high).astype(BF16).astype(F32)


def rows16(values):
    return jnp.concatenate(split2(values), 0).astype(BF16)


def spread(values):
    wide = jnp.concatenate([jnp.concatenate(split2(values), 0)] * OWN, 1)
    shape = (16, ROWS_DEV)
    keep = (iota(shape, 0) & 7) == (iota(shape, 1) >> 8)
    return jnp.where(keep, wide, 0.0).astype(BF16)


def own_part(wide):
    both = wide[:8] + wide[8:]
    row = iota((8, BLK), 0)
    total = jnp.zeros((8, BLK), F32)
    for n in range(OWN):
        total = total + jnp.where(row == n, both[:, n * BLK : (n + 1) * BLK], 0.0)
    return total


def halves(values):
    return jnp.concatenate([values[:8], values[8:]], 1)


def sum_all(values):
    folded = values[:, :128] + values[:, 128:]
    return jnp.broadcast_to(jnp.sum(folded, (0, 1), keepdims=True), (8, 128))


def wide(values):
    return jnp.concatenate([values, values], 1)


def column_of(row):
    return jnp.transpose(jnp.broadcast_to(row.astype(F32), (128, 128)))


def body(
    cfg_ref, order_ref, w_in_ref, bias_ref, w_out_ref, noise_ref, rhs_ref, nb_ref, live_ref, skel_ref,
    nb_s,
    x_out, r_out,
    grp_cfg, tiles, coup, own_feat, part_send, part_recv, skel_tiles, skel_cfg, pick, pick_t,
    msg_a, ret_send, ret_recv, quad, grp_q, grp_s,
    g_send, g_recv, s_send, s_recv, k_sem, it_sem,
):
    grp = lax.axis_index("grp")
    me = lax.axis_index("leaf")
    core = lax.rem(me, 2)
    xx = lax.rem(me // 2, 4)
    yy = me // 8

    def leaf_at(y, x, c):
        return lax.rem(y + 4, 4) * 8 + lax.rem(x + 4, 4) * 2 + c

    def leaf_peer(j):
        return lax.rem(me + j, N_LEAF)

    def grp_peer(j):
        return lax.rem(grp + j, N_GRP)

    barrier = pltpu.get_barrier_semaphore()

    def greet_leaf(j, _):
        pl.semaphore_signal(barrier, inc=1, device_id=(grp, leaf_peer(j)), device_id_type=MESH)
        return 0

    def greet_grp(j, _):
        pl.semaphore_signal(barrier, inc=1, device_id=(grp_peer(j), me), device_id_type=MESH)
        return 0

    lax.fori_loop(1, N_LEAF, greet_leaf, 0)
    lax.fori_loop(1, N_GRP, greet_grp, 0)

    def permute(b, _):
        row = order_ref[:, pl.ds(pl.multiple_of(b * BLK, BLK), BLK)]
        total = jnp.zeros((64, BLK), F32)
        for c in range(OWN):
            total = total + mm(cfg_ref[:, c * BLK : (c + 1) * BLK], one_hot(row, c * BLK))
        grp_cfg[me * OWN + b] = total.astype(BF16)
        return 0

    def at(half, first, second):
        return leaf_at(yy + second, xx + first, core) if half == 0 else leaf_at(yy + first, xx + second, core)

    def piece(leaf, half, quarter=None):
        if quarter is None:
            return grp_cfg.at[pl.ds(leaf * OWN + 4 * half, 4)]
        return grp_cfg.at[pl.ds(leaf * OWN + 4 * half + 2 * quarter, 2)]

    def hop(half, index, ref, target):
        return pltpu.make_async_remote_copy(
            src_ref=ref, dst_ref=ref, send_sem=g_send.at[half, index], recv_sem=g_recv.at[half, index],
            device_id=(grp, target), device_id_type=MESH,
        )

    sibling = me - core + lax.rem(core + 1, 2)

    def to_sibling(half, index, leaf):
        ref = piece(leaf, half)
        copy = pltpu.make_async_remote_copy(
            src_ref=ref, dst_ref=ref, send_sem=s_send.at[half, index], recv_sem=s_recv.at[half, index],
            device_id=(grp, sibling), device_id_type=MESH,
        )
        copy.start()
        return copy

    started = []

    def start(copy):
        copy.start()
        started.append(copy)

    offsets = (0, -1, 1, 2)

    def second_axis(half, p):
        ref = piece(at(half, offsets[p], 0), half)
        start(hop(half, 4 + 4 * p, ref, at(half, 0, 1)))
        start(hop(half, 5 + 4 * p, ref, at(half, 0, -1)))
        started.append(to_sibling(half, 4 * p, at(half, offsets[p], 0)))

    def arrived(half, index, ref):
        hop(half, index, ref, me).wait_recv()

    for half in range(2):
        lax.fori_loop(4 * half, 4 * half + 4, permute, 0)
        if half == 0:
            pl.semaphore_wait(barrier, N_LEAF - 1 + N_GRP - 1)
        own = piece(me, half)
        start(hop(half, 0, own, at(half, 1, 0)))
        start(hop(half, 1, own, at(half, -1, 0)))

    def choose(b, total):
        return total + mm(grp_cfg[me * OWN + b], one_hot(skel_ref[...] - me * ROWS_DEV, b * BLK))

    given = lax.fori_loop(0, OWN, choose, jnp.zeros((64, BLK), F32))
    for q in range(16):
        part_send[q] = given[q // 2 * 8 : q // 2 * 8 + 8, q % 2 * 128 : q % 2 * 128 + 128]
    part_recv[me] = part_send[me // 2]

    def send_part(j, _):
        peer = leaf_peer(j)
        pltpu.make_async_remote_copy(
            src_ref=part_send.at[peer // 2], dst_ref=part_recv.at[me], send_sem=k_sem.at[0], recv_sem=k_sem.at[1],
            device_id=(grp, peer), device_id_type=MESH,
        ).start()
        return 0

    lax.fori_loop(1, N_LEAF, send_part, 0)
    for half in range(2):
        second_axis(half, 0)

    w_in_t = flip(w_in_ref[...])
    w_out_t = flip(w_out_ref[...])
    bias = column_of(bias_ref[...])

    def features(configs):
        hidden = mm(w_in_t, configs)
        hidden = jnp.tanh(hidden + jnp.concatenate([bias] * (configs.shape[1] // 128), 1)).astype(BF16)
        raw = mm(w_out_t, hidden)
        return (raw * lax.rsqrt(jnp.sum(raw * raw, 0, keepdims=True) + 1e-06)).astype(BF16)

    def own_row(n, _):
        feat_t = features(grp_cfg[me * OWN + n])
        feat = flip(feat_t)
        own_feat[n] = feat
        tiles[NEAR + 1, pl.ds(n * BLK, BLK), :] = kernel_of(mm(feat, feat_t)).astype(BF16)
        return 0

    def sum_parts():
        many = part_recv.at[pl.ds(0, N_LEAF - 1)]
        pltpu.make_async_copy(many, many, k_sem.at[1]).wait()
        skel_tiles[me // 2] = jnp.sum(part_recv[...], 0)

        def send_tile(j, _):
            pltpu.make_async_remote_copy(
                src_ref=skel_tiles.at[me // 2], dst_ref=skel_tiles.at[me // 2], send_sem=k_sem.at[2], recv_sem=k_sem.at[3],
                device_id=(grp, leaf_peer(2 * j)), device_id_type=MESH,
            ).start()
            return 0

        lax.fori_loop(1, N_LEAF // 2, send_tile, 0)

    def send_skeleton():
        many = skel_tiles.at[pl.ds(0, N_LEAF // 2 - 1)]
        pltpu.make_async_copy(many, many, k_sem.at[3]).wait()
        for h in range(2):
            skel_cfg[grp, :, h * 128 : (h + 1) * 128] = jnp.concatenate(
                [skel_tiles[2 * q + h] for q in range(8)], 0
            ).astype(BF16)

        def send_skel(j, _):
            pltpu.make_async_remote_copy(
                src_ref=skel_cfg.at[grp], dst_ref=skel_cfg.at[grp], send_sem=k_sem.at[4], recv_sem=k_sem.at[5],
                device_id=(grp_peer(j), me), device_id_type=MESH,
            ).start()
            return 0

        lax.fori_loop(1, N_GRP, send_skel, 0)

    def use_skeletons():
        skel_t = features(skel_cfg[grp])

        def basis(n, _):
            tiles[NEAR, pl.ds(n * BLK, BLK), :] = kernel_of(mm(own_feat[n], skel_t)).astype(BF16)
            return 0

        lax.fori_loop(0, OWN, basis, 0)
        many = skel_cfg.at[pl.ds(0, N_GRP - 1)]
        pltpu.make_async_copy(many, many, k_sem.at[5]).wait()

        def couple(g, _):
            coup[pl.ds(g * BLK, BLK), :] = kernel_of(mm(flip(features(skel_cfg[g])), skel_t)).astype(BF16)
            return 0

        lax.fori_loop(0, N_GRP, couple, 0)

    lax.fori_loop(0, OWN, own_row, 0)
    for half in range(2):
        left, right = at(half, -1, 0), at(half, 1, 0)
        arrived(half, 0, piece(left, half))
        start(hop(half, 2, piece(left, half, 0), right))
        arrived(half, 1, piece(right, half))
        start(hop(half, 3, piece(right, half, 1), left))
    for half in range(2):
        second_axis(half, 1)
        second_axis(half, 2)
    sum_parts()
    for p in range(4):
        if p == 1:
            for half in range(2):
                far = at(half, 2, 0)
                arrived(half, 2, piece(far, half, 0))
                arrived(half, 3, piece(far, half, 1))
                second_axis(half, 3)
            send_skeleton()
        for half in range(2):
            down, up = at(half, offsets[p], -1), at(half, offsets[p], 1)
            arrived(half, 4 + 4 * p, piece(down, half))
            start(hop(half, 6 + 4 * p, piece(down, half, 0), at(half, 0, 1)))
            started.append(to_sibling(half, 4 * p + 1, down))
            arrived(half, 5 + 4 * p, piece(up, half))
            start(hop(half, 7 + 4 * p, piece(up, half, 1), at(half, 0, -1)))
            started.append(to_sibling(half, 4 * p + 2, up))
        if p == 3:
            use_skeletons()
        for half in range(2):
            over = at(half, offsets[p], 2)
            arrived(half, 6 + 4 * p, piece(over, half, 0))
            arrived(half, 7 + 4 * p, piece(over, half, 1))
            started.append(to_sibling(half, 4 * p + 3, over))
    steps = (0, -1, 1, 2)
    for p in range(4):
        for half in range(2):
            for s in range(4):
                theirs = at(half, offsets[p], steps[s]) - core + lax.rem(core + 1, 2)
                ref = piece(theirs, half)
                pltpu.make_async_remote_copy(
                    src_ref=ref, dst_ref=ref, send_sem=s_send.at[half, 4 * p + s], recv_sem=s_recv.at[half, 4 * p + s],
                    device_id=(grp, sibling), device_id_type=MESH,
                ).wait_recv()
    for copy in started:
        copy.wait_send()

    def tile_row(n, _):
        feat_t = features(jnp.concatenate([grp_cfg[nb_s[n, k]] for k in range(NEAR)], 1))
        made = kernel_of(mm(own_feat[n], feat_t)).astype(BF16)
        for k in range(NEAR):
            tiles[k, pl.ds(n * BLK, BLK), :] = made[:, k * BLK : (k + 1) * BLK]
        return 0

    lax.fori_loop(0, OWN, tile_row, 0)

    nb = nb_ref[...]
    live = live_ref[...].astype(F32)
    place = nb + (nb & -8)
    for h in range(2):
        for k in range(NEAR):
            hit = iota((8, 512), 1) == place[:, k : k + 1] + 8 * h
            pick[pl.ds((h * NEAR + k) * 8, 8), :] = jnp.where(hit, live[:, k : k + 1], 0.0)
    pick[pl.ds(96, 32), :] = jnp.zeros((32, 512), F32)
    for q in range(4):
        pick_t[pl.ds(q * 128, 128), :] = jnp.transpose(pick[:, q * 128 : (q + 1) * 128]).astype(BF16)
    count = jnp.zeros((8, BLK), F32)
    for k in range(NEAR):
        count = count + jnp.where(iota((8, BLK), 1) == nb[:, k : k + 1], live[:, k : k + 1], 0.0)
    count = jnp.sum(count, 0, keepdims=True)
    own_uses = jnp.sum(live, 1, keepdims=True)

    for index, sent in (
        (0, part_recv.at[pl.ds(0, N_LEAF - 1)]),
        (2, skel_tiles.at[pl.ds(0, N_LEAF // 2 - 1)]),
        (4, skel_cfg.at[pl.ds(0, N_GRP - 1)]),
    ):
        pltpu.make_async_copy(sent, sent, k_sem.at[index]).wait()

    noise = jnp.concatenate([noise_ref[pl.ds(0, 8, stride=2), :], noise_ref[pl.ds(1, 8, stride=2), :]], 1)
    right = jnp.concatenate([rhs_ref[pl.ds(0, 8, stride=2), :], rhs_ref[pl.ds(1, 8, stride=2), :]], 1)
    precond = 1.0 / (1.0 + noise)
    zero = jnp.zeros((8, BLK), F32)
    one = jnp.ones((8, 128), F32)

    def apply(t, v, dots, last):
        sem = it_sem.at[t]
        v_wide = spread(v)
        charge = jnp.sum(mm(v_wide, tiles[NEAR]), 0, keepdims=True)

        c_high, c_mid = split2(charge)
        rows = [c_high[:, :128], c_high[:, 128:], c_mid[:, :128], c_mid[:, 128:], count[:, :128], count[:, 128:]]
        lane = iota((8, 128), 1)
        sums = jnp.zeros((8, 128), F32)
        for index, values in enumerate(dots):
            sums = jnp.where(lane == index, sum_all(values), sums)
        s_high, s_mid = split2(sums)
        rows += [s_high[:1], s_mid[:1], (sums - s_high - s_mid)[:1]]
        row = iota((16, 128), 0)
        extra = jnp.zeros((16, 128), F32)
        for at_row, values in enumerate(rows):
            extra = jnp.where(row == at_row, values, extra)
        msg_a[t, me, pl.ds(0, 16), :] = jnp.concatenate([v[:, :128], v[:, 128:]], 0).astype(BF16)
        msg_a[t, me, pl.ds(16, 16), :] = extra.astype(BF16)

        def send_a(j, _):
            pltpu.make_async_remote_copy(
                src_ref=msg_a.at[t, me], dst_ref=msg_a.at[t, me], send_sem=sem.at[0], recv_sem=sem.at[1],
                device_id=(grp, leaf_peer(j)), device_id_type=MESH,
            ).start()
            return 0

        lax.fori_loop(1, N_LEAF, send_a, 0)

        backs = []
        for k in range(NEAR):
            made = mm(v_wide, tiles[k])
            backs.append(made[:8] + made[8:])
        stack = jnp.concatenate([b[:, :128] for b in backs] + [b[:, 128:] for b in backs] + [jnp.zeros((32, 128), F32)], 0)
        b_high, b_mid = split2(stack)
        returned = mm(pick_t[...], b_high.astype(BF16)) + mm(pick_t[...], b_mid.astype(BF16))
        ret_send[t] = returned.reshape(N_LEAF, 16, 128).astype(BF16)
        ret_recv[t, me] = ret_send[t, me]

        def send_r(j, _):
            peer = leaf_peer(j)
            pltpu.make_async_remote_copy(
                src_ref=ret_send.at[t, peer], dst_ref=ret_recv.at[t, me], send_sem=sem.at[2], recv_sem=sem.at[3],
                device_id=(grp, peer), device_id_type=MESH,
            ).start()
            return 0

        lax.fori_loop(1, N_LEAF, send_r, 0)
        made = mm(v_wide, tiles[NEAR + 1])
        self_part = made[:8] + made[8:]

        many = msg_a.at[t, pl.ds(0, N_LEAF - 1)]
        pltpu.make_async_copy(many, many, sem.at[1]).wait()
        extra = jnp.sum(msg_a[t, :, pl.ds(16, 16), :].astype(F32), 0)
        charge = jnp.concatenate([extra[0:1] + extra[2:3], extra[1:2] + extra[3:4]], 1)
        row = iota((8, 128), 0)
        tile = jnp.where(row == 0, charge[:, :128], 0.0)
        tile = jnp.where(row == 1, charge[:, 128:], tile)
        tile = jnp.where(row == 2, extra[6:7] + extra[7:8] + extra[8:9], tile)
        grp_q[t, grp] = tile

        def send_q(j, _):
            pltpu.make_async_remote_copy(
                src_ref=grp_q.at[t, grp], dst_ref=grp_q.at[t, grp], send_sem=sem.at[4], recv_sem=sem.at[5],
                device_id=(grp_peer(j), me), device_id_type=MESH,
            ).start()
            return 0

        lax.fori_loop(1, N_GRP, send_q, 0)

        counts = jnp.broadcast_to(jnp.concatenate([extra[4:5], extra[5:6]], 1), (8, BLK))
        mine = iota((8, BLK), 1) == me * OWN + iota((8, BLK), 0)
        weight = own_uses + jnp.sum(jnp.where(mine, counts, 0.0), 1, keepdims=True)
        self_part = weight * self_part
        vectors = msg_a[t, :, pl.ds(0, 16), :].reshape(N_LEAF * 16, 128)
        found = mm(pick[...].astype(BF16), vectors)
        partners = [
            jnp.concatenate([found[k * 8 : k * 8 + 8], found[(NEAR + k) * 8 : (NEAR + k) * 8 + 8]], 1) for k in range(NEAR)
        ]
        if last:
            share = v * (self_part + noise * v)
            for k in range(NEAR):
                share = share + 2.0 * backs[k] * partners[k]
            quad[me] = sum_all(share)[:1]

            def send_s(j, _):
                pltpu.make_async_remote_copy(
                    src_ref=quad.at[me], dst_ref=quad.at[me], send_sem=sem.at[6], recv_sem=sem.at[7],
                    device_id=(grp, leaf_peer(j)), device_id_type=MESH,
                ).start()
                return 0

            lax.fori_loop(1, N_LEAF, send_s, 0)

        forward = jnp.zeros((16, ROWS_DEV), F32)
        for k in range(NEAR):
            forward = forward + mm_t(jnp.concatenate([partners[k], zero], 0).astype(BF16), tiles[k])
        near = self_part + own_part(forward)
        many = ret_recv.at[t, pl.ds(0, N_LEAF - 1)]
        pltpu.make_async_copy(many, many, sem.at[3]).wait()
        near = near + halves(jnp.sum(ret_recv[t].astype(F32), 0)) + noise * v

        many = grp_q.at[t, pl.ds(0, N_GRP - 1)]
        pltpu.make_async_copy(many, many, sem.at[5]).wait()
        row = iota((8, BLK), 0)
        charges = zero
        sums = jnp.zeros((8, 128), F32)
        for g in range(N_GRP):
            tile = grp_q[t, g]
            charges = jnp.where(row == g, jnp.concatenate([tile[0:1], tile[1:2]], 1), charges)
            sums = sums + tile
        totals = [
            jnp.broadcast_to(jnp.sum(jnp.where(lane[:1] == index, sums[2:3], 0.0), 1, keepdims=True), (8, 128))
            for index in range(len(dots))
        ]
        field = jnp.sum(mm(spread(charges), coup[...]), 0, keepdims=True)
        if last:
            far_share = sum_all(jnp.where(row == 0, charge * field, 0.0))
            many = quad.at[pl.ds(0, N_LEAF - 1)]
            pltpu.make_async_copy(many, many, sem.at[7]).wait()
            grp_s[grp] = jnp.sum(quad[...], 0) + far_share[:1]

            def send_c(j, _):
                pltpu.make_async_remote_copy(
                    src_ref=grp_s.at[grp], dst_ref=grp_s.at[grp], send_sem=sem.at[8], recv_sem=sem.at[9],
                    device_id=(grp_peer(j), me), device_id_type=MESH,
                ).start()
                return 0

            lax.fori_loop(1, N_GRP, send_c, 0)
        far = own_part(mm_t(rows16(jnp.broadcast_to(field, (8, BLK))), tiles[NEAR]))
        quadratic = None
        if last:
            many = grp_s.at[pl.ds(0, N_GRP - 1)]
            pltpu.make_async_copy(many, many, sem.at[9]).wait()
            quadratic = jnp.broadcast_to(jnp.sum(grp_s[...], 0), (8, 128))
        waits = [
            (0, msg_a.at[t, pl.ds(0, N_LEAF - 1)]),
            (2, ret_recv.at[t, pl.ds(0, N_LEAF - 1)]),
            (4, grp_q.at[t, pl.ds(0, N_GRP - 1)]),
        ]
        if last:
            waits += [(6, quad.at[pl.ds(0, N_LEAF - 1)]), (8, grp_s.at[pl.ds(0, N_GRP - 1)])]
        for index, sent in waits:
            pltpu.make_async_copy(sent, sent, sem.at[index]).wait()
        return near + far, totals, quadratic

    def step(t, carry):
        x, r, p, s, z, w, gamma_old, energy_old = carry
        first = t == 0
        u = r * precond
        made, (gamma, delta, mixed), _ = apply(t, jnp.where(first, u, w * precond), (r * u, u * w, u * s), False)
        beta = jnp.where(t <= 1, jnp.zeros_like(gamma), gamma / gamma_old)
        energy = delta + 2.0 * beta * mixed + beta * beta * energy_old
        alpha = wide(jnp.where(first, jnp.zeros_like(gamma), gamma / energy))
        beta = wide(beta)
        p = jnp.where(first, zero, u + beta * p)
        s = jnp.where(first, zero, w + beta * s)
        z = jnp.where(first, zero, made + beta * z)
        w = jnp.where(first, made, w - alpha * z)
        return x + alpha * p, r - alpha * s, p, s, z, w, gamma, energy

    x, r, p, s, z, w, gamma_old, energy_old = lax.fori_loop(
        0, ITERS - 1, step, (zero, right, zero, zero, zero, zero, one, one)
    )
    u, m, q = r * precond, w * precond, s * precond
    made, sums, m_am = apply(
        ITERS - 1, m, (r * u, u * w, u * s, u * z, m * w, m * z, q * w, q * z, q * s), True
    )
    gamma, delta, mixed, uz, mw, mz, qw, qz, qs = sums
    beta = gamma / gamma_old
    energy = delta + 2.0 * beta * mixed + beta * beta * energy_old
    alpha = gamma / energy
    ss = mw + beta * (2.0 * qw + beta * qs)
    ru = delta + beta * mixed
    gamma_last = gamma - alpha * (2.0 * ru - alpha * ss)
    delta_last = delta - alpha * (2.0 * mw + beta * (uz + qw) - alpha * (m_am + beta * (2.0 * mz + beta * qz)))
    beta_last = gamma_last / gamma
    energy_last = delta_last + beta_last * (2.0 * (ru - alpha * ss) + beta_last * energy)
    alpha_last, alpha, beta, beta_last = (wide(a) for a in (gamma_last / energy_last, alpha, beta, beta_last))
    p = u + beta * p
    s = w + beta * s
    z = made + beta * z
    w = w - alpha * z
    x = x + alpha * p
    r = r - alpha * s
    p = r * precond + beta_last * p
    s = w + beta_last * s
    x = x + alpha_last * p
    r = r - alpha_last * s
    for ref, values in ((x_out, x), (r_out, r)):
        ref[pl.ds(0, 8, stride=2), :] = values[:, :128]
        ref[pl.ds(1, 8, stride=2), :] = values[:, 128:]


def on_device(
    configs, order, w_in, bias_in, w_out, noise, right_side, near_blocks, near_live, skeleton
):
    vmem = pl.BlockSpec(memory_space=pltpu.VMEM)
    smem = pl.BlockSpec(memory_space=pltpu.SMEM)
    dma = pltpu.SemaphoreType.DMA
    solution_, residual_ = pl.pallas_call(
        body,
        out_shape=[jax.ShapeDtypeStruct((16, 128), F32)] * 2,
        in_specs=[vmem] * 10 + [smem],
        out_specs=[vmem] * 2,
        scratch_shapes=[
            pltpu.VMEM((N_LEAF * OWN, 64, BLK), BF16),
            pltpu.VMEM((NEAR + 2, ROWS_DEV, BLK), BF16),
            pltpu.VMEM((N_GRP * BLK, BLK), BF16),
            pltpu.VMEM((OWN, BLK, 128), BF16),
            pltpu.VMEM((16, 8, 128), F32),
            pltpu.VMEM((N_LEAF, 8, 128), F32),
            pltpu.VMEM((16, 8, 128), F32),
            pltpu.VMEM((N_GRP, 64, BLK), BF16),
            pltpu.VMEM((128, 512), F32),
            pltpu.VMEM((512, 128), BF16),
            pltpu.VMEM((ITERS, N_LEAF, 32, 128), BF16),
            pltpu.VMEM((ITERS, N_LEAF, 16, 128), BF16),
            pltpu.VMEM((ITERS, N_LEAF, 16, 128), BF16),
            pltpu.VMEM((N_LEAF, 1, 128), F32),
            pltpu.VMEM((ITERS, N_GRP, 8, 128), F32),
            pltpu.VMEM((N_GRP, 1, 128), F32),
            dma((2, 20)),
            dma((2, 20)),
            dma((2, 16)),
            dma((2, 16)),
            dma((6,)),
            dma((ITERS, 10)),
        ],
        compiler_params=pltpu.CompilerParams(
            collective_id=0, has_side_effects=True, vmem_limit_bytes=56 * 2**20
        ),
        cost_estimate=pl.CostEstimate(flops=10**10, bytes_accessed=10**7, transcendentals=10**7),
    )(
        configs.T, order, w_in, bias_in.reshape(1, 128), w_out,
        noise.reshape(16, 128), right_side.reshape(16, 128), near_blocks, near_live, skeleton, near_blocks,
    )
    return solution_.reshape(-1), residual_.reshape(-1)


def solution(mesh):
    in_specs = (
        P(("grp", "leaf"), None),
        P(("grp", "leaf"), None),
        P(),
        P(),
        P(),
        P(("grp", "leaf")),
        P(("grp", "leaf")),
        P(("grp", "leaf"), None),
        P(("grp", "leaf"), None),
        P("grp", None),
    )
    out_specs = (P(("grp", "leaf")), P(("grp", "leaf")))
    return jax.shard_map(
        on_device, mesh=mesh, in_specs=in_specs, out_specs=out_specs, check_vma=False
    )
```

time: 142 us -> 113 us (0.80)
  Pallas kernels: 137 us -> 110 us
  local copies, waits for them, and re-layouts: 4.53 us -> 1.9 us
    pallas_call x1, Pallas kernels: 137 us -> 110 us  [on_device(): pl.pallas_call(body, out_shape=[jax.ShapeDtypeStruct((16, 128), F32)] * 2...]
    unnamed x7 -> x4, local copies, waits for them, and re-layouts: 4.53 us -> 1.9 us
where the time goes in v2:
time: 113 us
  Pallas kernels  110 us (97%)
  local copies, waits for them, and re-layouts  1.9 us (2%)
    pallas_call x1, Pallas kernels, on_device(): pl.pallas_call(body, out_shape=[jax.ShapeDtypeStruct((16, 128), F32)] * 2...  110 us

profile of v2, /device:TPU:1, one launch (start us, length us, event | category | flops | bytes accessed | tf_op | source)
XLA Modules:
  0.0 112.8 jit_solution(8064121245249691594)
XLA Ops:
  0.6 110.2 %shard_map.113 = (f32[16,128]{1,0:T(8,128)}, f32[16,128]{1,0:T(8,128)}) custom-call(bf16[64,2048]{1,0:T(8,128)(2,1)} %bitcast.8, s32[1,2048]{1,0:T(1,128)} %order_ref.1, bf16[64,128]{1,0:T(8,128)(2,1)} %w_in_ref.1, f32[1,128]{1,0:T(1,128)} %bitcast.11, bf16[128,128]{1,0:T(8,128)(2,1)} %w_out_ref.1, f32[16,128]{1,0:T(8,128)} %bitcast.9, f32[16,128]{1,0:T(8,128)} %bitcast.10, ...), custom_call_target="tpu_custom_call" | custom-call | flops 10000000000 | bytes 10000000 | tf_op jit(solution)/shard_map/pallas_call | solution.py:553
  110.9 0.0 copy-start
  110.9 1.3 %copy.14 = f32[2048]{0:T(1024)} copy(f32[2048]{0:T(1024)} %bitcast.7) | data formatting | bytes 16384
  112.2 0.0 copy-done
  112.2 0.6 copy.15
Async XLA Ops:
  110.9 1.3 %copy-start = (f32[16,128]{1,0:T(8,128)S(1)}, f32[16,128]{1,0:T(8,128)}, u32[]{:S(2)}) copy-start(f32[16,128]{1,0:T(8,128)} %get-tuple-element.5) | copy-start | bytes 24580

commit v3 on v2

--- a/solution.py
+++ b/solution.py
@@ -247,7 +247,7 @@
 
         lax.fori_loop(1, N_GRP, send_skel, 0)
 
-    def use_skeletons():
+    def make_basis():
         skel_t = features(skel_cfg[grp])
 
         def basis(n, _):
@@ -255,6 +255,9 @@
             return 0
 
         lax.fori_loop(0, OWN, basis, 0)
+        return skel_t
+
+    def make_couplings(skel_t):
         many = skel_cfg.at[pl.ds(0, N_GRP - 1)]
         pltpu.make_async_copy(many, many, k_sem.at[5]).wait()
 
@@ -263,6 +266,191 @@
             return 0
 
         lax.fori_loop(0, N_GRP, couple, 0)
+
+    nb = nb_ref[...]
+    live = live_ref[...].astype(F32)
+    place = nb + (nb & -8)
+    for h in range(2):
+        for k in range(NEAR):
+            hit = iota((8, 512), 1) == place[:, k : k + 1] + 8 * h
+            pick[pl.ds((h * NEAR + k) * 8, 8), :] = jnp.where(hit, live[:, k : k + 1], 0.0)
+    pick[pl.ds(96, 32), :] = jnp.zeros((32, 512), F32)
+    for q in range(4):
+        pick_t[pl.ds(q * 128, 128), :] = jnp.transpose(pick[:, q * 128 : (q + 1) * 128]).astype(BF16)
+    count = jnp.zeros((8, BLK), F32)
+    for k in range(NEAR):
+        count = count + jnp.where(iota((8, BLK), 1) == nb[:, k : k + 1], live[:, k : k + 1], 0.0)
+    count = jnp.sum(count, 0, keepdims=True)
+    own_uses = jnp.sum(live, 1, keepdims=True)
+
+    noise = jnp.concatenate([noise_ref[pl.ds(0, 8, stride=2), :], noise_ref[pl.ds(1, 8, stride=2), :]], 1)
+    target = jnp.concatenate([rhs_ref[pl.ds(0, 8, stride=2), :], rhs_ref[pl.ds(1, 8, stride=2), :]], 1)
+    precond = 1.0 / (1.0 + noise)
+    zero = jnp.zeros((8, BLK), F32)
+    one = jnp.ones((8, 128), F32)
+
+    def send_vector(t, v, dots):
+        sem = it_sem.at[t]
+        v_wide = spread(v)
+        charge = jnp.sum(mm(v_wide, tiles[NEAR]), 0, keepdims=True)
+
+        c_high, c_mid = split2(charge)
+        rows = [c_high[:, :128], c_high[:, 128:], c_mid[:, :128], c_mid[:, 128:], count[:, :128], count[:, 128:]]
+        lane = iota((8, 128), 1)
+        sums = jnp.zeros((8, 128), F32)
+        for index, values in enumerate(dots):
+            sums = jnp.where(lane == index, sum_all(values), sums)
+        s_high, s_mid = split2(sums)
+        rows += [s_high[:1], s_mid[:1], (sums - s_high - s_mid)[:1]]
+        row = iota((16, 128), 0)
+        extra = jnp.zeros((16, 128), F32)
+        for at_row, values in enumerate(rows):
+            extra = jnp.where(row == at_row, values, extra)
+        msg_a[t, me, pl.ds(0, 16), :] = jnp.concatenate([v[:, :128], v[:, 128:]], 0).astype(BF16)
+        msg_a[t, me, pl.ds(16, 16), :] = extra.astype(BF16)
+
+        def send_a(j, _):
+            pltpu.make_async_remote_copy(
+                src_ref=msg_a.at[t, me], dst_ref=msg_a.at[t, me], send_sem=sem.at[0], recv_sem=sem.at[1],
+                device_id=(grp, leaf_peer(j)), device_id_type=MESH,
+            ).start()
+            return 0
+
+        lax.fori_loop(1, N_LEAF, send_a, 0)
+        return v_wide
+
+    def send_returns(t, v_wide):
+        sem = it_sem.at[t]
+        backs = []
+        for k in range(NEAR):
+            made = mm(v_wide, tiles[k])
+            backs.append(made[:8] + made[8:])
+        stack = jnp.concatenate([b[:, :128] for b in backs] + [b[:, 128:] for b in backs] + [jnp.zeros((32, 128), F32)], 0)
+        b_high, b_mid = split2(stack)
+        returned = mm(pick_t[...], b_high.astype(BF16)) + mm(pick_t[...], b_mid.astype(BF16))
+        ret_send[t] = returned.reshape(N_LEAF, 16, 128).astype(BF16)
+        ret_recv[t, me] = ret_send[t, me]
+
+        def send_r(j, _):
+            peer = leaf_peer(j)
+            pltpu.make_async_remote_copy(
+                src_ref=ret_send.at[t, peer], dst_ref=ret_recv.at[t, me], send_sem=sem.at[2], recv_sem=sem.at[3],
+                device_id=(grp, peer), device_id_type=MESH,
+            ).start()
+            return 0
+
+        lax.fori_loop(1, N_LEAF, send_r, 0)
+        made = mm(v_wide, tiles[NEAR + 1])
+        return backs, made[:8] + made[8:]
+
+    def pass_charges(t):
+        sem = it_sem.at[t]
+        many = msg_a.at[t, pl.ds(0, N_LEAF - 1)]
+        pltpu.make_async_copy(many, many, sem.at[1]).wait()
+        extra = jnp.sum(msg_a[t, :, pl.ds(16, 16), :].astype(F32), 0)
+        charge = jnp.concatenate([extra[0:1] + extra[2:3], extra[1:2] + extra[3:4]], 1)
+        row = iota((8, 128), 0)
+        tile = jnp.where(row == 0, charge[:, :128], 0.0)
+        tile = jnp.where(row == 1, charge[:, 128:], tile)
+        tile = jnp.where(row == 2, extra[6:7] + extra[7:8] + extra[8:9], tile)
+        grp_q[t, grp] = tile
+
+        def send_q(j, _):
+            pltpu.make_async_remote_copy(
+                src_ref=grp_q.at[t, grp], dst_ref=grp_q.at[t, grp], send_sem=sem.at[4], recv_sem=sem.at[5],
+                device_id=(grp_peer(j), me), device_id_type=MESH,
+            ).start()
+            return 0
+
+        lax.fori_loop(1, N_GRP, send_q, 0)
+        return charge, extra
+
+    def finish(t, v, terms, group, n_dots, last):
+        sem = it_sem.at[t]
+        backs, self_part = terms
+        charge, extra = group
+        lane = iota((8, 128), 1)
+        counts = jnp.broadcast_to(jnp.concatenate([extra[4:5], extra[5:6]], 1), (8, BLK))
+        mine = iota((8, BLK), 1) == me * OWN + iota((8, BLK), 0)
+        weight = own_uses + jnp.sum(jnp.where(mine, counts, 0.0), 1, keepdims=True)
+        self_part = weight * self_part
+        vectors = msg_a[t, :, pl.ds(0, 16), :].reshape(N_LEAF * 16, 128)
+        found = mm(pick[...].astype(BF16), vectors)
+        partners = [
+            jnp.concatenate([found[k * 8 : k * 8 + 8], found[(NEAR + k) * 8 : (NEAR + k) * 8 + 8]], 1) for k in range(NEAR)
+        ]
+        if last:
+            share = v * (self_part + noise * v)
+            for k in range(NEAR):
+                share = share + 2.0 * backs[k] * partners[k]
+            quad[me] = sum_all(share)[:1]
+
+            def send_s(j, _):
+                pltpu.make_async_remote_copy(
+                    src_ref=quad.at[me], dst_ref=quad.at[me], send_sem=sem.at[6], recv_sem=sem.at[7],
+                    device_id=(grp, leaf_peer(j)), device_id_type=MESH,
+                ).start()
+                return 0
+
+            lax.fori_loop(1, N_LEAF, send_s, 0)
+
+        forward = jnp.zeros((16, ROWS_DEV), F32)
+        for k in range(NEAR):
+            forward = forward + mm_t(jnp.concatenate([partners[k], zero], 0).astype(BF16), tiles[k])
+        near = self_part + own_part(forward)
+        many = ret_recv.at[t, pl.ds(0, N_LEAF - 1)]
+        pltpu.make_async_copy(many, many, sem.at[3]).wait()
+        near = near + halves(jnp.sum(ret_recv[t].astype(F32), 0)) + noise * v
+
+        many = grp_q.at[t, pl.ds(0, N_GRP - 1)]
+        pltpu.make_async_copy(many, many, sem.at[5]).wait()
+        row = iota((8, BLK), 0)
+        charges = zero
+        sums = jnp.zeros((8, 128), F32)
+        for g in range(N_GRP):
+            tile = grp_q[t, g]
+            charges = jnp.where(row == g, jnp.concatenate([tile[0:1], tile[1:2]], 1), charges)
+            sums = sums + tile
+        totals = [
+            jnp.broadcast_to(jnp.sum(jnp.where(lane[:1] == index, sums[2:3], 0.0), 1, keepdims=True), (8, 128))
+            for index in range(n_dots)
+        ]
+        field = jnp.sum(mm(spread(charges), coup[...]), 0, keepdims=True)
+        if last:
+            far_share = sum_all(jnp.where(row == 0, charge * field, 0.0))
+            many = quad.at[pl.ds(0, N_LEAF - 1)]
+            pltpu.make_async_copy(many, many, sem.at[7]).wait()
+            grp_s[grp] = jnp.sum(quad[...], 0) + far_share[:1]
+
+            def send_c(j, _):
+                pltpu.make_async_remote_copy(
+                    src_ref=grp_s.at[grp], dst_ref=grp_s.at[grp], send_sem=sem.at[8], recv_sem=sem.at[9],
+                    device_id=(grp_peer(j), me), device_id_type=MESH,
+                ).start()
+                return 0
+
+            lax.fori_loop(1, N_GRP, send_c, 0)
+        far = own_part(mm_t(rows16(jnp.broadcast_to(field, (8, BLK))), tiles[NEAR]))
+        quadratic = None
+        if last:
+            many = grp_s.at[pl.ds(0, N_GRP - 1)]
+            pltpu.make_async_copy(many, many, sem.at[9]).wait()
+            quadratic = jnp.broadcast_to(jnp.sum(grp_s[...], 0), (8, 128))
+        waits = [
+            (0, msg_a.at[t, pl.ds(0, N_LEAF - 1)]),
+            (2, ret_recv.at[t, pl.ds(0, N_LEAF - 1)]),
+            (4, grp_q.at[t, pl.ds(0, N_GRP - 1)]),
+        ]
+        if last:
+            waits += [(6, quad.at[pl.ds(0, N_LEAF - 1)]), (8, grp_s.at[pl.ds(0, N_GRP - 1)])]
+        for index, sent in waits:
+            pltpu.make_async_copy(sent, sent, sem.at[index]).wait()
+        return near + far, totals, quadratic
+
+    def apply(t, v, dots, last):
+        v_wide = send_vector(t, v, dots)
+        terms = send_returns(t, v_wide)
+        return finish(t, v, terms, pass_charges(t), len(dots), last)
 
     lax.fori_loop(0, OWN, own_row, 0)
     for half in range(2):
@@ -291,13 +479,18 @@
             arrived(half, 5 + 4 * p, piece(up, half))
             start(hop(half, 7 + 4 * p, piece(up, half, 1), at(half, 0, -1)))
             started.append(to_sibling(half, 4 * p + 2, up))
+        if p == 2:
+            skel_t = make_basis()
+    for p in range(4):
         if p == 3:
-            use_skeletons()
+            make_couplings(skel_t)
         for half in range(2):
             over = at(half, offsets[p], 2)
             arrived(half, 6 + 4 * p, piece(over, half, 0))
             arrived(half, 7 + 4 * p, piece(over, half, 1))
             started.append(to_sibling(half, 4 * p + 3, over))
+    first = target * precond
+    first_wide = send_vector(0, first, ())
     steps = (0, -1, 1, 2)
     for p in range(4):
         for half in range(2):
@@ -319,22 +512,7 @@
         return 0
 
     lax.fori_loop(0, OWN, tile_row, 0)
-
-    nb = nb_ref[...]
-    live = live_ref[...].astype(F32)
-    place = nb + (nb & -8)
-    for h in range(2):
-        for k in range(NEAR):
-            hit = iota((8, 512), 1) == place[:, k : k + 1] + 8 * h
-            pick[pl.ds((h * NEAR + k) * 8, 8), :] = jnp.where(hit, live[:, k : k + 1], 0.0)
-    pick[pl.ds(96, 32), :] = jnp.zeros((32, 512), F32)
-    for q in range(4):
-        pick_t[pl.ds(q * 128, 128), :] = jnp.transpose(pick[:, q * 128 : (q + 1) * 128]).astype(BF16)
-    count = jnp.zeros((8, BLK), F32)
-    for k in range(NEAR):
-        count = count + jnp.where(iota((8, BLK), 1) == nb[:, k : k + 1], live[:, k : k + 1], 0.0)
-    count = jnp.sum(count, 0, keepdims=True)
-    own_uses = jnp.sum(live, 1, keepdims=True)
+    first_group = pass_charges(0)
 
     for index, sent in (
         (0, part_recv.at[pl.ds(0, N_LEAF - 1)]),
@@ -343,176 +521,23 @@
     ):
         pltpu.make_async_copy(sent, sent, k_sem.at[index]).wait()
 
-    noise = jnp.concatenate([noise_ref[pl.ds(0, 8, stride=2), :], noise_ref[pl.ds(1, 8, stride=2), :]], 1)
-    right = jnp.concatenate([rhs_ref[pl.ds(0, 8, stride=2), :], rhs_ref[pl.ds(1, 8, stride=2), :]], 1)
-    precond = 1.0 / (1.0 + noise)
-    zero = jnp.zeros((8, BLK), F32)
-    one = jnp.ones((8, 128), F32)
-
-    def apply(t, v, dots, last):
-        sem = it_sem.at[t]
-        v_wide = spread(v)
-        charge = jnp.sum(mm(v_wide, tiles[NEAR]), 0, keepdims=True)
-
-        c_high, c_mid = split2(charge)
-        rows = [c_high[:, :128], c_high[:, 128:], c_mid[:, :128], c_mid[:, 128:], count[:, :128], count[:, 128:]]
-        lane = iota((8, 128), 1)
-        sums = jnp.zeros((8, 128), F32)
-        for index, values in enumerate(dots):
-            sums = jnp.where(lane == index, sum_all(values), sums)
-        s_high, s_mid = split2(sums)
-        rows += [s_high[:1], s_mid[:1], (sums - s_high - s_mid)[:1]]
-        row = iota((16, 128), 0)
-        extra = jnp.zeros((16, 128), F32)
-        for at_row, values in enumerate(rows):
-            extra = jnp.where(row == at_row, values, extra)
-        msg_a[t, me, pl.ds(0, 16), :] = jnp.concatenate([v[:, :128], v[:, 128:]], 0).astype(BF16)
-        msg_a[t, me, pl.ds(16, 16), :] = extra.astype(BF16)
-
-        def send_a(j, _):
-            pltpu.make_async_remote_copy(
-                src_ref=msg_a.at[t, me], dst_ref=msg_a.at[t, me], send_sem=sem.at[0], recv_sem=sem.at[1],
-                device_id=(grp, leaf_peer(j)), device_id_type=MESH,
-            ).start()
-            return 0
-
-        lax.fori_loop(1, N_LEAF, send_a, 0)
-
-        backs = []
-        for k in range(NEAR):
-            made = mm(v_wide, tiles[k])
-            backs.append(made[:8] + made[8:])
-        stack = jnp.concatenate([b[:, :128] for b in backs] + [b[:, 128:] for b in backs] + [jnp.zeros((32, 128), F32)], 0)
-        b_high, b_mid = split2(stack)
-        returned = mm(pick_t[...], b_high.astype(BF16)) + mm(pick_t[...], b_mid.astype(BF16))
-        ret_send[t] = returned.reshape(N_LEAF, 16, 128).astype(BF16)
-        ret_recv[t, me] = ret_send[t, me]
-
-        def send_r(j, _):
-            peer = leaf_peer(j)
-            pltpu.make_async_remote_copy(
-                src_ref=ret_send.at[t, peer], dst_ref=ret_recv.at[t, me], send_sem=sem.at[2], recv_sem=sem.at[3],
-                device_id=(grp, peer), device_id_type=MESH,
-            ).start()
-            return 0
-
-        lax.fori_loop(1, N_LEAF, send_r, 0)
-        made = mm(v_wide, tiles[NEAR + 1])
-        self_part = made[:8] + made[8:]
-
-        many = msg_a.at[t, pl.ds(0, N_LEAF - 1)]
-        pltpu.make_async_copy(many, many, sem.at[1]).wait()
-        extra = jnp.sum(msg_a[t, :, pl.ds(16, 16), :].astype(F32), 0)
-        charge = jnp.concatenate([extra[0:1] + extra[2:3], extra[1:2] + extra[3:4]], 1)
-        row = iota((8, 128), 0)
-        tile = jnp.where(row == 0, charge[:, :128], 0.0)
-        tile = jnp.where(row == 1, charge[:, 128:], tile)
-        tile = jnp.where(row == 2, extra[6:7] + extra[7:8] + extra[8:9], tile)
-        grp_q[t, grp] = tile
-
-        def send_q(j, _):
-            pltpu.make_async_remote_copy(
-                src_ref=grp_q.at[t, grp], dst_ref=grp_q.at[t, grp], send_sem=sem.at[4], recv_sem=sem.at[5],
-                device_id=(grp_peer(j), me), device_id_type=MESH,
-            ).start()
-            return 0
-
-        lax.fori_loop(1, N_GRP, send_q, 0)
-
-        counts = jnp.broadcast_to(jnp.concatenate([extra[4:5], extra[5:6]], 1), (8, BLK))
-        mine = iota((8, BLK), 1) == me * OWN + iota((8, BLK), 0)
-        weight = own_uses + jnp.sum(jnp.where(mine, counts, 0.0), 1, keepdims=True)
-        self_part = weight * self_part
-        vectors = msg_a[t, :, pl.ds(0, 16), :].reshape(N_LEAF * 16, 128)
-        found = mm(pick[...].astype(BF16), vectors)
-        partners = [
-            jnp.concatenate([found[k * 8 : k * 8 + 8], found[(NEAR + k) * 8 : (NEAR + k) * 8 + 8]], 1) for k in range(NEAR)
-        ]
-        if last:
-            share = v * (self_part + noise * v)
-            for k in range(NEAR):
-                share = share + 2.0 * backs[k] * partners[k]
-            quad[me] = sum_all(share)[:1]
-
-            def send_s(j, _):
-                pltpu.make_async_remote_copy(
-                    src_ref=quad.at[me], dst_ref=quad.at[me], send_sem=sem.at[6], recv_sem=sem.at[7],
-                    device_id=(grp, leaf_peer(j)), device_id_type=MESH,
-                ).start()
-                return 0
-
-            lax.fori_loop(1, N_LEAF, send_s, 0)
-
-        forward = jnp.zeros((16, ROWS_DEV), F32)
-        for k in range(NEAR):
-            forward = forward + mm_t(jnp.concatenate([partners[k], zero], 0).astype(BF16), tiles[k])
-        near = self_part + own_part(forward)
-        many = ret_recv.at[t, pl.ds(0, N_LEAF - 1)]
-        pltpu.make_async_copy(many, many, sem.at[3]).wait()
-        near = near + halves(jnp.sum(ret_recv[t].astype(F32), 0)) + noise * v
-
-        many = grp_q.at[t, pl.ds(0, N_GRP - 1)]
-        pltpu.make_async_copy(many, many, sem.at[5]).wait()
-        row = iota((8, BLK), 0)
-        charges = zero
-        sums = jnp.zeros((8, 128), F32)
-        for g in range(N_GRP):
-            tile = grp_q[t, g]
-            charges = jnp.where(row == g, jnp.concatenate([tile[0:1], tile[1:2]], 1), charges)
-            sums = sums + tile
-        totals = [
-            jnp.broadcast_to(jnp.sum(jnp.where(lane[:1] == index, sums[2:3], 0.0), 1, keepdims=True), (8, 128))
-            for index in range(len(dots))
-        ]
-        field = jnp.sum(mm(spread(charges), coup[...]), 0, keepdims=True)
-        if last:
-            far_share = sum_all(jnp.where(row == 0, charge * field, 0.0))
-            many = quad.at[pl.ds(0, N_LEAF - 1)]
-            pltpu.make_async_copy(many, many, sem.at[7]).wait()
-            grp_s[grp] = jnp.sum(quad[...], 0) + far_share[:1]
-
-            def send_c(j, _):
-                pltpu.make_async_remote_copy(
-                    src_ref=grp_s.at[grp], dst_ref=grp_s.at[grp], send_sem=sem.at[8], recv_sem=sem.at[9],
-                    device_id=(grp_peer(j), me), device_id_type=MESH,
-                ).start()
-                return 0
-
-            lax.fori_loop(1, N_GRP, send_c, 0)
-        far = own_part(mm_t(rows16(jnp.broadcast_to(field, (8, BLK))), tiles[NEAR]))
-        quadratic = None
-        if last:
-            many = grp_s.at[pl.ds(0, N_GRP - 1)]
-            pltpu.make_async_copy(many, many, sem.at[9]).wait()
-            quadratic = jnp.broadcast_to(jnp.sum(grp_s[...], 0), (8, 128))
-        waits = [
-            (0, msg_a.at[t, pl.ds(0, N_LEAF - 1)]),
-            (2, ret_recv.at[t, pl.ds(0, N_LEAF - 1)]),
-            (4, grp_q.at[t, pl.ds(0, N_GRP - 1)]),
-        ]
-        if last:
-            waits += [(6, quad.at[pl.ds(0, N_LEAF - 1)]), (8, grp_s.at[pl.ds(0, N_GRP - 1)])]
-        for index, sent in waits:
-            pltpu.make_async_copy(sent, sent, sem.at[index]).wait()
-        return near + far, totals, quadratic
+    w, _, _ = finish(0, first, send_returns(0, first_wide), first_group, 0, False)
 
     def step(t, carry):
         x, r, p, s, z, w, gamma_old, energy_old = carry
-        first = t == 0
         u = r * precond
-        made, (gamma, delta, mixed), _ = apply(t, jnp.where(first, u, w * precond), (r * u, u * w, u * s), False)
-        beta = jnp.where(t <= 1, jnp.zeros_like(gamma), gamma / gamma_old)
+        made, (gamma, delta, mixed), _ = apply(t, w * precond, (r * u, u * w, u * s), False)
+        beta = jnp.where(t == 1, jnp.zeros_like(gamma), gamma / gamma_old)
         energy = delta + 2.0 * beta * mixed + beta * beta * energy_old
-        alpha = wide(jnp.where(first, jnp.zeros_like(gamma), gamma / energy))
+        alpha = wide(gamma / energy)
         beta = wide(beta)
-        p = jnp.where(first, zero, u + beta * p)
-        s = jnp.where(first, zero, w + beta * s)
-        z = jnp.where(first, zero, made + beta * z)
-        w = jnp.where(first, made, w - alpha * z)
-        return x + alpha * p, r - alpha * s, p, s, z, w, gamma, energy
+        p = u + beta * p
+        s = w + beta * s
+        z = made + beta * z
+        return x + alpha * p, r - alpha * s, p, s, z, w - alpha * z, gamma, energy
 
     x, r, p, s, z, w, gamma_old, energy_old = lax.fori_loop(
-        0, ITERS - 1, step, (zero, right, zero, zero, zero, zero, one, one)
+        1, ITERS - 1, step, (zero, target, zero, zero, zero, w, one, one)
     )
     u, m, q = r * precond, w * precond, s * precond
     made, sums, m_am = apply(

time: 113 us -> 104 us (0.920)
  Pallas kernels: 110 us -> 101 us
    pallas_call x1, Pallas kernels: 110 us -> 101 us  [on_device(): pl.pallas_call(body, out_shape=[jax.ShapeDtypeStruct((16, 128), F32)] * 2...]
where the time goes in v3:
time: 104 us
  Pallas kernels  101 us (97%)
  local copies, waits for them, and re-layouts  1.9 us (2%)
    pallas_call x1, Pallas kernels, on_device(): pl.pallas_call(body, out_shape=[jax.ShapeDtypeStruct((16, 128), F32)] * 2...  101 us

profile of v3, /device:TPU:1, one launch (start us, length us, event | category | flops | bytes accessed | tf_op | source)
XLA Modules:
  0.0 103.8 jit_solution(12723798313414704737)
XLA Ops:
  0.6 101.3 %shard_map.113 = (f32[16,128]{1,0:T(8,128)}, f32[16,128]{1,0:T(8,128)}) custom-call(bf16[64,2048]{1,0:T(8,128)(2,1)} %bitcast.8, s32[1,2048]{1,0:T(1,128)} %order_ref.1, bf16[64,128]{1,0:T(8,128)(2,1)} %w_in_ref.1, f32[1,128]{1,0:T(1,128)} %bitcast.11, bf16[128,128]{1,0:T(8,128)(2,1)} %w_out_ref.1, f32[16,128]{1,0:T(8,128)} %bitcast.9, f32[16,128]{1,0:T(8,128)} %bitcast.10, ...), custom_call_target="tpu_custom_call" | custom-call | flops 10000000000 | bytes 10000000 | tf_op jit(solution)/shard_map/pallas_call | solution.py:578
  101.9 0.0 copy-start
  101.9 1.3 %copy.14 = f32[2048]{0:T(1024)} copy(f32[2048]{0:T(1024)} %bitcast.7) | data formatting | bytes 16384
  103.2 0.0 copy-done
  103.2 0.6 copy.15
Async XLA Ops:
  101.9 1.3 %copy-start = (f32[16,128]{1,0:T(8,128)S(1)}, f32[16,128]{1,0:T(8,128)}, u32[]{:S(2)}) copy-start(f32[16,128]{1,0:T(8,128)} %get-tuple-element.5) | copy-start | bytes 24580

commit v4 on v3

--- a/solution.py
+++ b/solution.py
@@ -88,9 +88,9 @@
 def body(
     cfg_ref, order_ref, w_in_ref, bias_ref, w_out_ref, noise_ref, rhs_ref, nb_ref, live_ref, skel_ref,
     nb_s,
-    x_out, r_out,
+    xr_out,
     grp_cfg, tiles, coup, own_feat, part_send, part_recv, skel_tiles, skel_cfg, pick, pick_t,
-    msg_a, ret_send, ret_recv, quad, grp_q, grp_s,
+    msg_q, msg_v, ret_send, ret_recv, quad, grp_q, grp_s,
     g_send, g_recv, s_send, s_recv, k_sem, it_sem,
 ):
     grp = lax.axis_index("grp")
@@ -306,17 +306,18 @@
         extra = jnp.zeros((16, 128), F32)
         for at_row, values in enumerate(rows):
             extra = jnp.where(row == at_row, values, extra)
-        msg_a[t, me, pl.ds(0, 16), :] = jnp.concatenate([v[:, :128], v[:, 128:]], 0).astype(BF16)
-        msg_a[t, me, pl.ds(16, 16), :] = extra.astype(BF16)
-
-        def send_a(j, _):
-            pltpu.make_async_remote_copy(
-                src_ref=msg_a.at[t, me], dst_ref=msg_a.at[t, me], send_sem=sem.at[0], recv_sem=sem.at[1],
-                device_id=(grp, leaf_peer(j)), device_id_type=MESH,
-            ).start()
-            return 0
-
-        lax.fori_loop(1, N_LEAF, send_a, 0)
+        msg_q[t, me] = extra.astype(BF16)
+        msg_v[t, me] = jnp.concatenate([v[:, :128], v[:, 128:]], 0).astype(BF16)
+        for ref, index in ((msg_q, 0), (msg_v, 10)):
+
+            def send_a(j, _, ref=ref, index=index):
+                pltpu.make_async_remote_copy(
+                    src_ref=ref.at[t, me], dst_ref=ref.at[t, me], send_sem=sem.at[index], recv_sem=sem.at[index + 1],
+                    device_id=(grp, leaf_peer(j)), device_id_type=MESH,
+                ).start()
+                return 0
+
+            lax.fori_loop(1, N_LEAF, send_a, 0)
         return v_wide
 
     def send_returns(t, v_wide):
@@ -345,9 +346,9 @@
 
     def pass_charges(t):
         sem = it_sem.at[t]
-        many = msg_a.at[t, pl.ds(0, N_LEAF - 1)]
+        many = msg_q.at[t, pl.ds(0, N_LEAF - 1)]
         pltpu.make_async_copy(many, many, sem.at[1]).wait()
-        extra = jnp.sum(msg_a[t, :, pl.ds(16, 16), :].astype(F32), 0)
+        extra = jnp.sum(msg_q[t].astype(F32), 0)
         charge = jnp.concatenate([extra[0:1] + extra[2:3], extra[1:2] + extra[3:4]], 1)
         row = iota((8, 128), 0)
         tile = jnp.where(row == 0, charge[:, :128], 0.0)
@@ -374,7 +375,9 @@
         mine = iota((8, BLK), 1) == me * OWN + iota((8, BLK), 0)
         weight = own_uses + jnp.sum(jnp.where(mine, counts, 0.0), 1, keepdims=True)
         self_part = weight * self_part
-        vectors = msg_a[t, :, pl.ds(0, 16), :].reshape(N_LEAF * 16, 128)
+        many = msg_v.at[t, pl.ds(0, N_LEAF - 1)]
+        pltpu.make_async_copy(many, many, sem.at[11]).wait()
+        vectors = msg_v[t].reshape(N_LEAF * 16, 128)
         found = mm(pick[...].astype(BF16), vectors)
         partners = [
             jnp.concatenate([found[k * 8 : k * 8 + 8], found[(NEAR + k) * 8 : (NEAR + k) * 8 + 8]], 1) for k in range(NEAR)
@@ -437,7 +440,8 @@
             pltpu.make_async_copy(many, many, sem.at[9]).wait()
             quadratic = jnp.broadcast_to(jnp.sum(grp_s[...], 0), (8, 128))
         waits = [
-            (0, msg_a.at[t, pl.ds(0, N_LEAF - 1)]),
+            (0, msg_q.at[t, pl.ds(0, N_LEAF - 1)]),
+            (10, msg_v.at[t, pl.ds(0, N_LEAF - 1)]),
             (2, ret_recv.at[t, pl.ds(0, N_LEAF - 1)]),
             (4, grp_q.at[t, pl.ds(0, N_GRP - 1)]),
         ]
@@ -464,12 +468,13 @@
         second_axis(half, 2)
     sum_parts()
     for p in range(4):
-        if p == 1:
+        if p == 0:
             for half in range(2):
                 far = at(half, 2, 0)
                 arrived(half, 2, piece(far, half, 0))
                 arrived(half, 3, piece(far, half, 1))
                 second_axis(half, 3)
+        if p == 1:
             send_skeleton()
         for half in range(2):
             down, up = at(half, offsets[p], -1), at(half, offsets[p], 1)
@@ -564,9 +569,9 @@
     s = w + beta_last * s
     x = x + alpha_last * p
     r = r - alpha_last * s
-    for ref, values in ((x_out, x), (r_out, r)):
-        ref[pl.ds(0, 8, stride=2), :] = values[:, :128]
-        ref[pl.ds(1, 8, stride=2), :] = values[:, 128:]
+    for base, values in ((0, x), (16, r)):
+        xr_out[pl.ds(base, 8, stride=2), :] = values[:, :128]
+        xr_out[pl.ds(base + 1, 8, stride=2), :] = values[:, 128:]
 
 
 def on_device(
@@ -575,11 +580,11 @@
     vmem = pl.BlockSpec(memory_space=pltpu.VMEM)
     smem = pl.BlockSpec(memory_space=pltpu.SMEM)
     dma = pltpu.SemaphoreType.DMA
-    solution_, residual_ = pl.pallas_call(
+    both = pl.pallas_call(
         body,
-        out_shape=[jax.ShapeDtypeStruct((16, 128), F32)] * 2,
+        out_shape=jax.ShapeDtypeStruct((32, 128), F32),
         in_specs=[vmem] * 10 + [smem],
-        out_specs=[vmem] * 2,
+        out_specs=vmem,
         scratch_shapes=[
             pltpu.VMEM((N_LEAF * OWN, 64, BLK), BF16),
             pltpu.VMEM((NEAR + 2, ROWS_DEV, BLK), BF16),
@@ -591,7 +596,8 @@
             pltpu.VMEM((N_GRP, 64, BLK), BF16),
             pltpu.VMEM((128, 512), F32),
             pltpu.VMEM((512, 128), BF16),
-            pltpu.VMEM((ITERS, N_LEAF, 32, 128), BF16),
+            pltpu.VMEM((ITERS, N_LEAF, 16, 128), BF16),
+            pltpu.VMEM((ITERS, N_LEAF, 16, 128), BF16),
             pltpu.VMEM((ITERS, N_LEAF, 16, 128), BF16),
             pltpu.VMEM((ITERS, N_LEAF, 16, 128), BF16),
             pltpu.VMEM((N_LEAF, 1, 128), F32),
@@ -602,7 +608,7 @@
             dma((2, 16)),
             dma((2, 16)),
             dma((6,)),
-            dma((ITERS, 10)),
+            dma((ITERS, 12)),
         ],
         compiler_params=pltpu.CompilerParams(
             collective_id=0, has_side_effects=True, vmem_limit_bytes=56 * 2**20
@@ -612,7 +618,7 @@
         configs.T, order, w_in, bias_in.reshape(1, 128), w_out,
         noise.reshape(16, 128), right_side.reshape(16, 128), near_blocks, near_live, skeleton, near_blocks,
     )
-    return solution_.reshape(-1), residual_.reshape(-1)
+    return both[:16].reshape(-1), both[16:].reshape(-1)
 
 
 def solution(mesh):

time: 104 us -> 101 us (0.971)
  Pallas kernels: 101 us -> 99.1 us
    pallas_call x1, Pallas kernels: 101 us -> 99.1 us  [on_device(): pl.pallas_call(body, out_shape=jax.ShapeDtypeStruct((32, 128), F32), in_s...]
    unnamed x4 -> x0, local copies, waits for them, and re-layouts: 1.9 us -> none
    reshape x0 -> x1, local copies, waits for them, and re-layouts: none -> 1.32 us  [on_device(): return (both[:16].reshape(-1), both[16:].reshape(-1))]
where the time goes in v4:
time: 101 us
  Pallas kernels  99.1 us (98%)
  local copies, waits for them, and re-layouts  1.32 us (1%)
    pallas_call x1, Pallas kernels, on_device(): pl.pallas_call(body, out_shape=jax.ShapeDtypeStruct((32, 128), F32), in_s...  99.1 us

profile of v4, /device:TPU:1, one launch (start us, length us, event | category | flops | bytes accessed | tf_op | source)
XLA Modules:
  0.0 101.0 jit_solution(8626301169392660497)
XLA Ops:
  0.6 99.1 %shard_map.113 = f32[32,128]{1,0:T(8,128)} custom-call(bf16[64,2048]{1,0:T(8,128)(2,1)} %bitcast.8, s32[1,2048]{1,0:T(1,128)} %order_ref.1, bf16[64,128]{1,0:T(8,128)(2,1)} %w_in_ref.1, f32[1,128]{1,0:T(1,128)} %bitcast.11, bf16[128,128]{1,0:T(8,128)(2,1)} %w_out_ref.1, f32[16,128]{1,0:T(8,128)} %bitcast.9, f32[16,128]{1,0:T(8,128)} %bitcast.10, ...), custom_call_target="tpu_custom_call" | custom-call | flops 10000000000 | bytes 10000000 | tf_op jit(solution)/shard_map/pallas_call | solution.py:583
  99.7 1.3 %slice_bitcast_fusion = (f32[2048]{0:T(1024)}, f32[2048]{0:T(1024)}) fusion(f32[32,128]{1,0:T(8,128)} %shard_map.113), kind=kLoop, calls=%fused_computation | loop fusion | bytes 32768 | tf_op jit(solution)/shard_map/reshape | solution.py:621

commit v5 on v4

--- a/solution.py
+++ b/solution.py
@@ -487,8 +487,6 @@
         if p == 2:
             skel_t = make_basis()
     for p in range(4):
-        if p == 3:
-            make_couplings(skel_t)
         for half in range(2):
             over = at(half, offsets[p], 2)
             arrived(half, 6 + 4 * p, piece(over, half, 0))
@@ -526,7 +524,9 @@
     ):
         pltpu.make_async_copy(sent, sent, k_sem.at[index]).wait()
 
-    w, _, _ = finish(0, first, send_returns(0, first_wide), first_group, 0, False)
+    first_terms = send_returns(0, first_wide)
+    make_couplings(skel_t)
+    w, _, _ = finish(0, first, first_terms, first_group, 0, False)
 
     def step(t, carry):
         x, r, p, s, z, w, gamma_old, energy_old = carry

time: 101 us -> 98.3 us (0.973)
  Pallas kernels: 99.1 us -> 96.2 us
    pallas_call x1, Pallas kernels: 99.1 us -> 96.2 us  [on_device(): pl.pallas_call(body, out_shape=jax.ShapeDtypeStruct((32, 128), F32), in_s...]
where the time goes in v5:
time: 98.3 us; the launch traced here: 98.1 us
  Pallas kernels  96.2 us (98%)
  local copies, waits for them, and re-layouts  1.32 us (1%)
    pallas_call x1, Pallas kernels, on_device(): pl.pallas_call(body, out_shape=jax.ShapeDtypeStruct((32, 128), F32), in_s...  96.2 us

profile of v5, /device:TPU:1, one launch (start us, length us, event | category | flops | bytes accessed | tf_op | source)
XLA Modules:
  0.0 98.1 jit_solution(12533873076601764192)
XLA Ops:
  0.6 96.2 %shard_map.113 = f32[32,128]{1,0:T(8,128)} custom-call(bf16[64,2048]{1,0:T(8,128)(2,1)} %bitcast.8, s32[1,2048]{1,0:T(1,128)} %order_ref.1, bf16[64,128]{1,0:T(8,128)(2,1)} %w_in_ref.1, f32[1,128]{1,0:T(1,128)} %bitcast.11, bf16[128,128]{1,0:T(8,128)(2,1)} %w_out_ref.1, f32[16,128]{1,0:T(8,128)} %bitcast.9, f32[16,128]{1,0:T(8,128)} %bitcast.10, ...), custom_call_target="tpu_custom_call" | custom-call | flops 10000000000 | bytes 10000000 | tf_op jit(solution)/shard_map/pallas_call | solution.py:583
  96.8 1.3 %slice_bitcast_fusion = (f32[2048]{0:T(1024)}, f32[2048]{0:T(1024)}) fusion(f32[32,128]{1,0:T(8,128)} %shard_map.113), kind=kLoop, calls=%fused_computation | loop fusion | bytes 32768 | tf_op jit(solution)/shard_map/reshape | solution.py:621
